TPU v7x, 128 devices: a whole 4x4x4 slice. The times are simulated.
128 devices in a mesh: attn: 16 (over y, x), ffn: 8 (over z, core).
Axes of the slice: x: 4, y: 4, z: 4, core: 2. Of those that a mesh axis runs over, the one named last changes fastest.
Arguments:
- hidden: bfloat16 [2048, 7168], P(('attn', 'ffn')), may hold values from -6 to 6
- norm_gain: float32 [7168], replicated, may hold values from 0.1 to 1.9
- expert_ids: int32 [2048, 3], P(('attn', 'ffn')), may hold values from 0 to 7, all different within a row; in each aligned block of 16 rows (0 to 15, 16 to 31, ...) at most 8 rows name the same one
- gate_scores: float32 [2048, 3], P(('attn', 'ffn')), may hold values from 0.1 to 0.6
- expert_in: bfloat16 [8, 2, 5120, 7168], P('ffn', None, 'attn'), may hold values from -0.0625 to 0.0625
- expert_out: bfloat16 [8, 5120, 7168], P('ffn', 'attn'), may hold values from -0.078125 to 0.078125
- kv_pages: bfloat16 [4096, 64, 512], P(('attn', 'ffn')), may hold values from -6 to 6
- block_table: int32 [2048, 2], P(('attn', 'ffn')), may hold values from 0 to 31, as said below
- req_len: int32 [2048], P(('attn', 'ffn')), may hold values from 1 to 128
- new_owner: int32 [2048, 1], P(('attn', 'ffn')), may hold values from 0 to 15; in each aligned block of 16 rows (0 to 15, 16 to 31, ...) at most 2 rows name the same one
Outputs:
- moved_pages: bfloat16 [4096, 2, 64, 512], P(('attn', 'ffn'))
- moved_rows: bfloat16 [4096, 7168], P(('attn', 'ffn'))
Inputs may be any that keep to these rules, and one draw needn't show every extreme that they name: `expert_ids`: each row names 3 different experts; at most 8 rows of one device name the same expert, and some device has exactly 8 rows on one expert. `new_owner`: at most 2 rows of one device name the same instance, and some device has exactly 2 rows on one instance. `block_table`: the entries of the 16 rows of one device name each of that device's 16 * 2 local page slots once.
All inputs are finite; a program needn't handle non-finite values.
Results may differ from a plain program's by a relative error of at most 0.011.
Values may be sent and summed in bfloat16 or wider, within the bound.
No kernel may reach another device: no remote copies, remote signals or barrier semaphores. Data moves between devices by JAX's collectives and lax.ppermute only.
A program may use at most 128 MiB of HBM per device.

v0:
```python
import jax
import jax.numpy as jnp
from jax import lax
from jax.sharding import PartitionSpec as P

PAGE = 64
PAGES_REQ = 2


def body(
    hidden,
    norm_gain,
    expert_ids,
    gate_scores,
    expert_in,
    expert_out,
    kv_pages,
    block_table,
    req_len,
    new_owner,
):
    req_dev = hidden.shape[0]
    width = hidden.shape[1]
    topk = expert_ids.shape[1]
    members = lax.axis_size("ffn")
    instances = lax.axis_size("attn")
    expert_cap = req_dev * topk * 4 // (members * 3)
    per_peer = 2 * req_dev // instances
    owners = new_owner.reshape(-1)
    owner_hot = (owners[:, None] == jnp.arange(instances, dtype=jnp.int32)[None, :]).astype(
        jnp.int32
    )
    owner_rank = jnp.sum((jnp.cumsum(owner_hot, axis=0) - owner_hot) * owner_hot, axis=1)
    send_slot = owners * per_peer + owner_rank
    routing = jnp.arange(instances * per_peer, dtype=jnp.int32)[:, None] == send_slot[None, :]
    occupied = jnp.any(routing, axis=1)
    sources = jnp.sum(
        routing.astype(jnp.int32) * jnp.arange(req_dev, dtype=jnp.int32)[None, :], axis=1
    )
    tables = block_table[sources]
    page_rows = kv_pages[tables]
    positions = (
        jnp.arange(PAGES_REQ, dtype=jnp.int32)[:, None] * PAGE
        + jnp.arange(PAGE, dtype=jnp.int32)[None, :]
    )
    kept_mask = (positions[None, :, :] < req_len[sources][:, None, None]) & occupied[:, None, None]
    outgoing_pages = jnp.where(kept_mask[..., None], page_rows, jnp.zeros_like(page_rows))
    floats = hidden.astype(jnp.float32)
    scale = lax.rsqrt(jnp.mean(floats * floats, axis=-1, keepdims=True) + 1e-06)
    normed = (floats * scale * norm_gain).astype(jnp.bfloat16)
    pair_ids = expert_ids.reshape(-1)
    onehot = (pair_ids[:, None] == jnp.arange(members, dtype=jnp.int32)[None, :]).astype(jnp.int32)
    rank_pos = jnp.sum((jnp.cumsum(onehot, axis=0) - onehot) * onehot, axis=1)
    slot_ids = pair_ids * expert_cap + rank_pos
    matches = jnp.arange(members * expert_cap, dtype=jnp.int32)[:, None] == slot_ids[None, :]
    matches = matches.reshape(members * expert_cap, req_dev, topk)
    picker = jnp.sum(matches.astype(jnp.int32), axis=2).astype(jnp.bfloat16)
    outgoing = jnp.dot(picker, normed, preferred_element_type=jnp.float32).astype(jnp.bfloat16)
    arrived = lax.all_to_all(
        outgoing.reshape(members, expert_cap, width), "ffn", split_axis=0, concat_axis=0, tiled=True
    )
    arrived = arrived.reshape(members * expert_cap, width)
    hidden_dev = expert_in.shape[2]
    weight_in = expert_in.reshape(2 * hidden_dev, width)
    weight_out = expert_out.reshape(hidden_dev, width)
    gate_up = lax.dot_general(
        lax.all_gather(arrived, "attn", axis=0, tiled=True),
        weight_in,
        (((1,), (1,)), ((), ())),
        preferred_element_type=jnp.float32,
    )
    activated = (jax.nn.silu(gate_up[:, :hidden_dev]) * gate_up[:, hidden_dev:]).astype(
        jnp.bfloat16
    )
    summed = lax.psum_scatter(
        jnp.dot(activated, weight_out, preferred_element_type=jnp.float32).astype(jnp.bfloat16),
        "attn",
        scatter_dimension=0,
        tiled=True,
    )
    results = summed.reshape(members, expert_cap, width)
    returned = lax.all_to_all(results, "ffn", split_axis=0, concat_axis=0, tiled=True)
    combine_weights = jnp.einsum(
        "sjk,jk->js", matches.astype(jnp.float32), gate_scores, precision=lax.Precision.HIGHEST
    )
    expert_mix = jnp.dot(
        combine_weights,
        returned.reshape(members * expert_cap, width).astype(jnp.float32),
        precision=lax.Precision.HIGHEST,
    )
    updated = (floats + expert_mix).astype(jnp.bfloat16)
    rows_out = jnp.dot(
        routing.astype(jnp.bfloat16), updated, preferred_element_type=jnp.float32
    ).astype(jnp.bfloat16)
    moved_pages, moved_rows = (
        lax.all_to_all(outgoing_pages, "attn", split_axis=0, concat_axis=0, tiled=True),
        lax.all_to_all(rows_out, "attn", split_axis=0, concat_axis=0, tiled=True),
    )
    return (moved_pages, moved_rows)


def solution(mesh):
    in_specs = (
        P(("attn", "ffn"), None),
        P(),
        P(("attn", "ffn"), None),
        P(("attn", "ffn"), None),
        P("ffn", None, "attn", None),
        P("ffn", "attn", None),
        P(("attn", "ffn"), None, None),
        P(("attn", "ffn"), None),
        P(("attn", "ffn")),
        P(("attn", "ffn"), None),
    )
    out_specs = (P(("attn", "ffn"), None, None, None), P(("attn", "ffn"), None))
    return jax.shard_map(body, mesh=mesh, in_specs=in_specs, out_specs=out_specs, check_vma=False)
```

profile of v0, /device:TPU:0, one launch (start us, length us, event | category | flops | bytes accessed | tf_op | source)
XLA Modules:
  0.0 372.4 jit_solution(1619637013816432624)
XLA Ops:
  7.2 0.9 copy.31
  8.4 0.2 select_reduce_fusion
  8.6 0.1 copy.32
  8.7 0.7 multiply_add_fusion
  9.5 1.1 fusion.7
  10.6 1.4 fusion
  12.0 20.0 %all_to_all.27 = bf16[8,8,7168]{2,1,0:T(8,128)(2,1)} all-to-all(bf16[8,8,7168]{2,1,0:T(8,128)(2,1)S(1)} %fusion), channel_id=1, replica_groups=mesh['attn'=16,'ffn'=8] {'ffn'}, dimensions={0} | all-to-all | bytes 1835008 | tf_op jit(solution)/shard_map/all_to_all | solution.py:59
  32.0 100.1 %all-gather.2.cloned.1.call-done = bf16[1024,7168]{1,0:T(8,128)(2,1)} async-done(((bf16[64,7168]{1,0:T(8,128)(2,1)}), bf16[1024,7168]{1,0:T(8,128)(2,1)}) %all-gather.2.cloned.1.call-update) | async-done | bytes 14680080 | tf_op jit(solution)/shard_map/all_gather | solution.py:67
  132.1 14.5 %fusion.22 = f32[1024,640]{0,1:T(8,128)S(1)} fusion(bf16[1024,7168]{1,0:T(8,128)(2,1)} %all-gather.2.cloned.1.call-done, bf16[640,7168]{1,0:T(8,128)(2,1)} %bitcast.37), kind=kOutput, calls=%fused_computation.49 | convolution fusion | flops 9395240960 | bytes 26476544 | tf_op jit(solution)/shard_map/dot_general | solution.py:66
  146.6 11.3 %convolution_convert_fusion = bf16[1024,7168]{1,0:T(8,128)(2,1)} fusion(bf16[1,320,7168]{2,1,0:T(8,128)(2,1)S(1)} %bitcast.39, f32[1024,640]{0,1:T(8,128)S(1)} %fusion.22), kind=kOutput, calls=%fused_computation.3 | convolution fusion | flops 4706926592 | bytes 21889024 | tf_op jit(solution)/shard_map/dot_general | solution.py:76
  157.9 0.6 copy-done.4
  158.8 0.2 select_reduce_fusion.2
  159.0 0.1 select_reduce_fusion.1
  159.1 0.6 gather_fusion.1
  159.7 0.1 copy.30
  159.8 0.1 reshape.142
  160.0 99.2 %reduce-scatter.2.cloned.1.call-done = bf16[64,7168]{1,0:T(8,128)(2,1)} async-done(((bf16[1024,7168]{1,0:T(8,128)(2,1)}), bf16[64,7168]{1,0:T(8,128)(2,1)}) %reduce-scatter.2.cloned.1.call-update) | async-done | bytes 917520 | tf_op jit(solution)/shard_map/reduce_scatter | solution.py:75
  259.2 4.4 %all-to-all-start.2 = ((bf16[8,8,7168]{2,1,0:T(8,128)(2,1)}), bf16[8,8,7168]{2,1,0:T(8,128)(2,1)S(1)}, u32[]{:S(2)}, u32[]{:S(2)}) async-start(bf16[8,8,7168]{2,1,0:T(8,128)(2,1)} %bitcast.32), calls=%async_computation.3 | async-start | bytes 1835008 | tf_op jit(solution)/shard_map/all_to_all | solution.py:82
  263.6 0.7 gather_fusion
  264.3 2.8 gather_fusion.2
  267.3 0.1 compare_and_fusion
  267.4 4.0 %broadcast_select_fusion = bf16[32,2,64,512]{3,2,1,0:T(8,128)(2,1)} fusion(bf16[32,2,64,512]{3,2,1,0:T(8,128)(2,1)} %bitcast.30, pred[32,2,64]{2,1,0:T(4,128)(4,1)S(1)} %compare_and_fusion), kind=kLoop, calls=%fused_computation.10 | loop fusion | flops 2097152 | bytes 8392704 | tf_op jit(solution)/shard_map/jit(_where)/select_n | solution.py:47
  271.4 6.8 %all-to-all-done.2 = bf16[8,8,7168]{2,1,0:T(8,128)(2,1)S(1)} async-done(((bf16[8,8,7168]{2,1,0:T(8,128)(2,1)}), bf16[8,8,7168]{2,1,0:T(8,128)(2,1)S(1)}, u32[]{:S(2)}, u32[]{:S(2)}) %all-to-all-start.2) | async-done | bytes 917536 | tf_op jit(solution)/shard_map/all_to_all | solution.py:82
  278.2 4.6 %all-to-all-start = ((bf16[32,2,64,512]{3,2,1,0:T(8,128)(2,1)}), bf16[32,2,64,512]{3,2,1,0:T(8,128)(2,1)}, u32[]{:S(2)}, u32[]{:S(2)}) async-start(bf16[32,2,64,512]{3,2,1,0:T(8,128)(2,1)} %broadcast_select_fusion), calls=%async_computation | async-start | bytes 8388608 | tf_op jit(solution)/shard_map/all_to_all | solution.py:96
  283.0 0.2 fusion.13
  283.2 0.5 fusion.1
  283.7 0.4 convolution_convert_fusion.2
  284.1 0.2 all_to_all.20
  284.3 61.6 %all-to-all-done = bf16[32,2,64,512]{3,2,1,0:T(8,128)(2,1)} async-done(((bf16[32,2,64,512]{3,2,1,0:T(8,128)(2,1)}), bf16[32,2,64,512]{3,2,1,0:T(8,128)(2,1)}, u32[]{:S(2)}, u32[]{:S(2)}) %all-to-all-start) | async-done | bytes 4194336 | tf_op jit(solution)/shard_map/all_to_all | solution.py:96
  345.8 14.1 %all_to_all.28 = bf16[16,2,7168]{2,1,0:T(2,128)(2,1)S(1)} all-to-all(bf16[16,2,7168]{2,1,0:T(2,128)(2,1)S(1)} %all_to_all.20), channel_id=1, replica_groups=mesh['attn'=16,'ffn'=8] {'attn'}, dimensions={0} | all-to-all | bytes 917504 | tf_op jit(solution)/shard_map/all_to_all | solution.py:97
  359.9 0.9 all_to_all.22
  360.8 4.7 %copy.39 = bf16[32,2,64,512]{3,2,1,0:T(8,128)(2,1)} copy(bf16[32,2,64,512]{3,2,1,0:T(8,128)(2,1)} %all-to-all-done) | data formatting | bytes 8388608
  (40 shorter events, 1.2 us)
Async XLA Ops:
  7.2 257.2 %copy-start = (bf16[32,64,512]{2,1,0:T(8,128)(2,1)S(1)}, bf16[32,64,512]{2,1,0:T(8,128)(2,1)}, u32[]{:S(2)}) copy-start(bf16[32,64,512]{2,1,0:T(8,128)(2,1)} %param.16) | copy-start | bytes 6291460
  7.2 125.0 %all-gather.2.cloned.1.call-start = ((), (), s32[]{:S(2)}) async-start(), calls=%async_computation.5 | async-start | bytes 15597568 | tf_op jit(solution)/shard_map/all_gather | solution.py:67
  32.0 114.6 %slice-start = ((s8[4587520]{0:T(1024)(128)(4,1)}), s8[393216]{0:T(1024)(128)(4,1)S(1)}, s32[]{:S(2)}) async-start(s8[4587520]{0:T(1024)(128)(4,1)} %bitcast.38), calls=%async_computation.7 | async-start | bytes 786432
  32.0 227.2 %reduce-scatter.2.cloned.1.call-start = ((), (), s32[]{:S(2)}) async-start(), calls=%async_computation.6 | async-start | bytes 15597568 | tf_op jit(solution)/shard_map/reduce_scatter | solution.py:75
  132.1 14.5 %slice-start.1 = ((s8[4587520]{0:T(1024)(128)(4,1)}), s8[4194304]{0:T(1024)(128)(4,1)S(1)}, s32[]{:S(2)}) async-start(s8[4587520]{0:T(1024)(128)(4,1)} %bitcast.38), calls=%async_computation.8 | async-start | bytes 8388608
  157.9 0.7 copy-start.4
  157.9 0.8 copy-start.5
  157.9 105.7 %copy-start.1 = (s32[16]{0:T(128)S(1)}, s32[16]{0:T(128)}, u32[]{:S(2)}) copy-start(s32[16]{0:T(128)} %param.18) | copy-start | bytes 196
  259.2 19.0 %all-to-all-start.2 = ((bf16[8,8,7168]{2,1,0:T(8,128)(2,1)}), bf16[8,8,7168]{2,1,0:T(8,128)(2,1)S(1)}, u32[]{:S(2)}, u32[]{:S(2)}) async-start(bf16[8,8,7168]{2,1,0:T(8,128)(2,1)} %bitcast.32), calls=%async_computation.3 | async-start | bytes 1835008 | tf_op jit(solution)/shard_map/all_to_all | solution.py:82
  271.4 11.5 %copy-start.3 = (f32[16,3]{0,1:T(4,128)S(1)}, f32[16,3]{0,1:T(4,128)}, u32[]{:S(2)}) copy-start(f32[16,3]{0,1:T(4,128)} %param.13) | copy-start | bytes 580
  271.4 11.8 %copy-start.2 = (bf16[16,7168]{1,0:T(8,128)(2,1)S(1)}, bf16[16,7168]{1,0:T(8,128)(2,1)}, u32[]{:S(2)}) copy-start(bf16[16,7168]{1,0:T(8,128)(2,1)} %param.10) | copy-start | bytes 688132
  278.2 67.6 %all-to-all-start = ((bf16[32,2,64,512]{3,2,1,0:T(8,128)(2,1)}), bf16[32,2,64,512]{3,2,1,0:T(8,128)(2,1)}, u32[]{:S(2)}, u32[]{:S(2)}) async-start(bf16[32,2,64,512]{3,2,1,0:T(8,128)(2,1)} %broadcast_select_fusion), calls=%async_computation | async-start | bytes 8388608 | tf_op jit(solution)/shard_map/all_to_all | solution.py:96
Sparse Core Ops, SparseCore 0:
  32.1 99.9 all-gather.1
  158.1 101.0 reduce-scatter.1
where the time goes:
time: 373 us; the launch traced here: 372 us
  waiting for transfers between devices  268 us (72%)
  blocking collectives  34 us (9%)
  matrix products  28.2 us (8%)
  between operations  14.2 us (4%)
  local copies, waits for them, and re-layouts  12.2 us (3%)
  starting transfers between devices  9.13 us (2%)
  other arithmetic  6.97 us (2%)
    all_gather x1, waiting for transfers between devices, body(): lax.all_gather(arrived, 'attn', axis=0, tiled=True)  100 us
    reduce_scatter x1, waiting for transfers between devices, body(): lax.psum_scatter(jnp.dot(activated, weight_out, preferred_element_type=jn...  99.2 us
    all_to_all x1, waiting for transfers between devices, body(): lax.all_to_all(outgoing_pages, 'attn', split_axis=0, concat_axis=0, tiled...  61.6 us
    all_to_all x1, blocking collectives, body(): lax.all_to_all(outgoing.reshape(members, expert_cap, width), 'ffn', split...  20 us
    dot_general x1, matrix products, body(): lax.dot_general(lax.all_gather(arrived, 'attn', axis=0, tiled=True), weig...  14.5 us
    all_to_all x1, blocking collectives, body(): lax.all_to_all(rows_out, 'attn', split_axis=0, concat_axis=0, tiled=True)  14.1 us
    dot_general x1, matrix products, body(): jnp.dot(activated, weight_out, preferred_element_type=jnp.float32)  11.3 us
  transfers between devices with their start and end apart: 4, of which 4 were waited for; matrix products, arithmetic and copies ran while one was open for 3% of the time, Pallas kernels for 0%

commit v1 on v0

v1 whole, which is shorter than its diff:
```python
import functools

import jax
import jax.numpy as jnp
from jax import lax
from jax.experimental import pallas as pl
from jax.experimental.pallas import tpu as pltpu
from jax.sharding import PartitionSpec as P

PAGE = 64
PAGES_REQ = 2
ID_LANES = 128
MIB = 1 << 20


def expert_kernel(width, hidden_dev, req_dev, cap, member_ref, rows_ref, win_ref, wout_ref, out_ref, acc_ref):
    rows = rows_ref.shape[0]
    slots = out_ref.shape[0]
    chunk = 1024
    acc_ref[...] = jnp.zeros_like(acc_ref)

    def up(step, carry):
        cols = pl.ds(pl.multiple_of(step * chunk, chunk), chunk)
        acc_ref[...] += lax.dot_general(
            rows_ref[:, cols],
            win_ref[:, cols],
            (((1,), (1,)), ((), ())),
            preferred_element_type=jnp.float32,
        )
        return carry

    lax.fori_loop(0, width // chunk, up, 0)
    gate = acc_ref[:, :hidden_dev]
    act = (gate / (1.0 + jnp.exp(-gate)) * acc_ref[:, hidden_dev : 2 * hidden_dev]).astype(jnp.bfloat16)
    ids = rows_ref[:, width : width + ID_LANES].astype(jnp.float32)
    member = member_ref[0].astype(jnp.float32)
    hit = jnp.max(jnp.where(ids == member, 1.0, 0.0), axis=1, keepdims=True)
    first = lax.broadcasted_iota(jnp.int32, (rows, rows), 0)
    second = lax.broadcasted_iota(jnp.int32, (rows, rows), 1)
    before = jnp.where((second < first) & (second // req_dev == first // req_dev), 1.0, 0.0)
    rank = jnp.dot(
        before.astype(jnp.bfloat16),
        jnp.broadcast_to(hit, (rows, 128)).astype(jnp.bfloat16),
        preferred_element_type=jnp.float32,
    )[:, :1]
    block = lax.broadcasted_iota(jnp.int32, (rows, 1), 0) // req_dev
    place = jnp.where(hit > 0.0, block * cap + rank.astype(jnp.int32), -1)
    chosen = jnp.where(place == lax.broadcasted_iota(jnp.int32, (rows, slots), 1), 1.0, 0.0)
    picked = jnp.dot(
        jnp.transpose(chosen).astype(jnp.bfloat16), act, preferred_element_type=jnp.float32
    ).astype(jnp.bfloat16)

    def down(step, carry):
        cols = pl.ds(pl.multiple_of(step * chunk, chunk), chunk)
        out_ref[:, cols] = jnp.dot(
            picked, wout_ref[:, cols], preferred_element_type=jnp.float32
        ).astype(out_ref.dtype)
        return carry

    lax.fori_loop(0, width // chunk, down, 0)


def run_experts(member, rows, weight_in, weight_out, req_dev, cap, devices):
    width = weight_in.shape[1]
    hidden_dev = weight_out.shape[0]
    steps = 4
    block = rows.shape[0] // steps
    slots = devices * cap // steps
    once = pl.Buffered(1)
    return pl.pallas_call(
        functools.partial(expert_kernel, width, hidden_dev, req_dev, cap),
        out_shape=jax.ShapeDtypeStruct((devices * cap, width), jnp.bfloat16),
        grid=(steps,),
        in_specs=[
            pl.BlockSpec(memory_space=pltpu.SMEM),
            pl.BlockSpec((block, rows.shape[1]), lambda s: (s, 0)),
            pl.BlockSpec(weight_in.shape, lambda s: (0, 0), pipeline_mode=once),
            pl.BlockSpec(weight_out.shape, lambda s: (0, 0), pipeline_mode=once),
        ],
        out_specs=pl.BlockSpec((slots, width), lambda s: (s, 0)),
        scratch_shapes=[pltpu.VMEM((block, 2 * hidden_dev), jnp.float32)],
        compiler_params=pltpu.CompilerParams(vmem_limit_bytes=56 * MIB),
        cost_estimate=pl.CostEstimate(
            flops=2 * rows.shape[0] * width * 2 * hidden_dev + 2 * devices * cap * width * hidden_dev,
            bytes_accessed=2 * (rows.size + weight_in.size + weight_out.size + devices * cap * width),
            transcendentals=rows.shape[0] * hidden_dev,
        ),
    )(member, rows, weight_in, weight_out)


def body(
    hidden,
    norm_gain,
    expert_ids,
    gate_scores,
    expert_in,
    expert_out,
    kv_pages,
    block_table,
    req_len,
    new_owner,
):
    req_dev = hidden.shape[0]
    width = hidden.shape[1]
    topk = expert_ids.shape[1]
    members = lax.axis_size("ffn")
    instances = lax.axis_size("attn")
    expert_cap = req_dev * topk * 4 // (members * 3)
    per_peer = 2 * req_dev // instances

    floats = hidden.astype(jnp.float32)
    scale = lax.rsqrt(jnp.mean(floats * floats, axis=-1, keepdims=True) + 1e-06)
    normed = (floats * scale * norm_gain).astype(jnp.bfloat16)
    id_lanes = jnp.pad(expert_ids, ((0, 0), (0, ID_LANES - topk)), constant_values=-1)
    payload = jnp.concatenate([normed, id_lanes.astype(jnp.bfloat16)], axis=1)
    payload, kv_pages = lax.optimization_barrier((payload, kv_pages))
    gathered = lax.all_gather(payload, ("attn", "ffn"), axis=0, tiled=True)

    owners = new_owner.reshape(-1)
    owner_hot = (owners[:, None] == jnp.arange(instances, dtype=jnp.int32)[None, :]).astype(
        jnp.int32
    )
    owner_rank = jnp.sum((jnp.cumsum(owner_hot, axis=0) - owner_hot) * owner_hot, axis=1)
    send_slot = owners * per_peer + owner_rank
    routing = jnp.arange(instances * per_peer, dtype=jnp.int32)[:, None] == send_slot[None, :]
    occupied = jnp.any(routing, axis=1)
    sources = jnp.sum(
        routing.astype(jnp.int32) * jnp.arange(req_dev, dtype=jnp.int32)[None, :], axis=1
    )
    tables = block_table[sources]
    page_rows = kv_pages[tables]
    positions = (
        jnp.arange(PAGES_REQ, dtype=jnp.int32)[:, None] * PAGE
        + jnp.arange(PAGE, dtype=jnp.int32)[None, :]
    )
    kept_mask = (positions[None, :, :] < req_len[sources][:, None, None]) & occupied[:, None, None]
    outgoing_pages = jnp.where(kept_mask[..., None], page_rows, jnp.zeros_like(page_rows))
    moved_pages = lax.all_to_all(outgoing_pages, "attn", split_axis=0, concat_axis=0, tiled=True)

    gathered, moved_pages = lax.optimization_barrier((gathered, moved_pages))
    member = lax.axis_index("ffn").astype(jnp.int32).reshape(1)
    hidden_dev = expert_in.shape[2]
    partial = run_experts(
        member,
        gathered,
        expert_in.reshape(2 * hidden_dev, width),
        expert_out.reshape(hidden_dev, width),
        req_dev,
        expert_cap,
        members * instances,
    )
    summed = lax.psum_scatter(partial, "attn", scatter_dimension=0, tiled=True)
    results = summed.reshape(members, expert_cap, width)
    returned = lax.all_to_all(results, "ffn", split_axis=0, concat_axis=0, tiled=True)

    pair_ids = expert_ids.reshape(-1)
    onehot = (pair_ids[:, None] == jnp.arange(members, dtype=jnp.int32)[None, :]).astype(jnp.int32)
    rank_pos = jnp.sum((jnp.cumsum(onehot, axis=0) - onehot) * onehot, axis=1)
    slot_ids = pair_ids * expert_cap + rank_pos
    matches = jnp.arange(members * expert_cap, dtype=jnp.int32)[:, None] == slot_ids[None, :]
    matches = matches.reshape(members * expert_cap, req_dev, topk)
    combine_weights = jnp.einsum(
        "sjk,jk->js", matches.astype(jnp.float32), gate_scores, precision=lax.Precision.HIGHEST
    )
    expert_mix = jnp.dot(
        combine_weights,
        returned.reshape(members * expert_cap, width).astype(jnp.float32),
        precision=lax.Precision.HIGHEST,
    )
    updated = (floats + expert_mix).astype(jnp.bfloat16)
    rows_out = jnp.dot(
        routing.astype(jnp.bfloat16), updated, preferred_element_type=jnp.float32
    ).astype(jnp.bfloat16)
    moved_rows = lax.all_to_all(rows_out, "attn", split_axis=0, concat_axis=0, tiled=True)
    return (moved_pages, moved_rows)


def solution(mesh):
    in_specs = (
        P(("attn", "ffn"), None),
        P(),
        P(("attn", "ffn"), None),
        P(("attn", "ffn"), None),
        P("ffn", None, "attn", None),
        P("ffn", "attn", None),
        P(("attn", "ffn"), None, None),
        P(("attn", "ffn"), None),
        P(("attn", "ffn")),
        P(("attn", "ffn"), None),
    )
    out_specs = (P(("attn", "ffn"), None, None, None), P(("attn", "ffn"), None))
    return jax.shard_map(body, mesh=mesh, in_specs=in_specs, out_specs=out_specs, check_vma=False)
```

time: 373 us -> 358 us (0.960)
  Pallas kernels: 0 us -> 53.8 us
  blocking collectives: 34 us -> 0 us
  matrix products: 28.2 us -> 0.92 us
  waiting for transfers between devices: 268 us -> 249 us
  starting transfers between devices: 9.13 us -> 16.3 us
  other arithmetic: 6.97 us -> 10.9 us
    pallas_call x0 -> x1, Pallas kernels: none -> 53.8 us  [run_experts(): pl.pallas_call(functools.partial(expert_kernel, width, hidden_dev, req_de...]
    all_gather x1, waiting for transfers between devices: 100 us -> 51.8 us  [body(): gathered = lax.all_gather(payload, ('attn', 'ffn'), axis=0, tiled=True)]
    all_to_all x2 -> x0, blocking collectives: 34 us -> none  [the longest x1 20 us: body(): lax.all_to_all(outgoing.reshape(members, expert_cap, width), 'ffn', split...]
    dot_general x4 -> x0, matrix products: 27.3 us -> none  [the longest x1 14.5 us: body(): lax.dot_general(lax.all_gather(arrived, 'attn', axis=0, tiled=True), weig...]
    all_to_all x0 -> x1, waiting for transfers between devices: none -> 10.6 us  [body(): lax.all_to_all(rows_out, 'attn', split_axis=0, concat_axis=0, tiled=True)]
    all_to_all x1, waiting for transfers between devices: 61.6 us -> 71.8 us  [body(): lax.all_to_all(outgoing_pages, 'attn', split_axis=0, concat_axis=0, tiled...]
    all_to_all x1, waiting for transfers between devices: 6.82 us -> 13.6 us  [body(): lax.all_to_all(results, 'ffn', split_axis=0, concat_axis=0, tiled=True)]
    all_to_all x0 -> x1, starting transfers between devices: none -> 4.61 us  [body(): lax.all_to_all(rows_out, 'attn', split_axis=0, concat_axis=0, tiled=True)]
  transfers between devices with their start and end apart: 4 -> 5, of which waited for: 4 -> 5; matrix products, arithmetic and copies ran while one was open for 3% -> 4% of each run, Pallas kernels for 0% -> 0%
where the time goes in v1:
time: 358 us
  waiting for transfers between devices  249 us (70%)
  Pallas kernels  53.8 us (15%)
  starting transfers between devices  16.3 us (5%)
  between operations  14.1 us (4%)
  local copies, waits for them, and re-layouts  12.9 us (4%)
  other arithmetic  10.9 us (3%)
    reduce_scatter x1, waiting for transfers between devices, body(): summed = lax.psum_scatter(partial, 'attn', scatter_dimension=0, tiled=True)  101 us
    all_to_all x1, waiting for transfers between devices, body(): lax.all_to_all(outgoing_pages, 'attn', split_axis=0, concat_axis=0, tiled...  71.8 us
    pallas_call x1, Pallas kernels, run_experts(): pl.pallas_call(functools.partial(expert_kernel, width, hidden_dev, req_de...  53.8 us
    all_gather x1, waiting for transfers between devices, body(): gathered = lax.all_gather(payload, ('attn', 'ffn'), axis=0, tiled=True)  51.8 us
    all_to_all x1, waiting for transfers between devices, body(): lax.all_to_all(results, 'ffn', split_axis=0, concat_axis=0, tiled=True)  13.6 us
    all_to_all x1, waiting for transfers between devices, body(): lax.all_to_all(rows_out, 'attn', split_axis=0, concat_axis=0, tiled=True)  10.6 us
    all_to_all x1, starting transfers between devices, body(): lax.all_to_all(outgoing_pages, 'attn', split_axis=0, concat_axis=0, tiled...  7.17 us
  transfers between devices with their start and end apart: 5, of which 5 were waited for; matrix products, arithmetic and copies ran while one was open for 4% of the time, Pallas kernels for 0%

profile of v1, /device:TPU:0, one launch (start us, length us, event | category | flops | bytes accessed | tf_op | source)
XLA Modules:
  0.0 357.8 jit_solution(5788831234959017849)
XLA Ops:
  7.2 1.2 fusion.4
  8.5 0.7 convert.4
  9.2 0.1 copy.30
  9.3 1.1 fusion.6
  10.3 0.7 fusion.7
  11.1 0.8 copy.31
  11.8 0.7 fusion.9
  12.6 0.8 select_reduce_fusion.3
  13.4 0.7 multiply_add_fusion.1
  14.2 1.4 gather_fusion
  15.6 0.6 gather_fusion.1
  16.2 0.1 copy.33
  16.3 0.1 reshape.138
  16.5 2.8 gather_fusion.2
  19.4 0.1 compare_and_fusion
  19.6 4.0 %broadcast_select_fusion = bf16[32,2,64,512]{3,2,1,0:T(8,128)(2,1)} fusion(bf16[32,2,64,512]{3,2,1,0:T(8,128)(2,1)} %bitcast.24, pred[32,2,64]{2,1,0:T(4,128)(4,1)S(1)} %compare_and_fusion), kind=kLoop, calls=%fused_computation.6 | loop fusion | flops 2097152 | bytes 8392704 | tf_op jit(solution)/shard_map/jit(_where)/select_n | solution.py:137
  23.5 7.2 %all-to-all-start = ((bf16[32,2,64,512]{3,2,1,0:T(8,128)(2,1)}), bf16[32,2,64,512]{3,2,1,0:T(8,128)(2,1)}, u32[]{:S(2)}, u32[]{:S(2)}) async-start(bf16[32,2,64,512]{3,2,1,0:T(8,128)(2,1)} %broadcast_select_fusion), calls=%async_computation | async-start | bytes 8388608 | tf_op jit(solution)/shard_map/all_to_all | solution.py:138
  30.8 71.8 %all-to-all-done = bf16[32,2,64,512]{3,2,1,0:T(8,128)(2,1)} async-done(((bf16[32,2,64,512]{3,2,1,0:T(8,128)(2,1)}), bf16[32,2,64,512]{3,2,1,0:T(8,128)(2,1)}, u32[]{:S(2)}, u32[]{:S(2)}) %all-to-all-start) | async-done | bytes 4194336 | tf_op jit(solution)/shard_map/all_to_all | solution.py:138
  102.6 51.8 %all-gather.2.cloned.1.call-done.rows_ref = bf16[2048,7296]{1,0:T(8,128)(2,1)} async-done(((bf16[16,7296]{1,0:T(8,128)(2,1)}), bf16[2048,7296]{1,0:T(8,128)(2,1)}) %all-gather.2.cloned.1.call-update) | async-done | bytes 29884432 | tf_op jit(solution)/shard_map/all_gather | solution.py:117
  154.4 53.8 %shard_map.113 = bf16[1024,7168]{1,0:T(8,128)(2,1)} custom-call(s32[1]{0:T(128)} %bitcast.6.member_ref, bf16[2048,7296]{1,0:T(8,128)(2,1)} %all-gather.2.cloned.1.call-done.rows_ref, bf16[640,7168]{1,0:T(8,128)(2,1)} %bitcast.28, bf16[320,7168]{1,0:T(8,128)(2,1)} %bitcast.29), custom_call_target="tpu_custom_call" | custom-call | flops 23488102400 | bytes 58327040 | tf_op jit(solution)/shard_map/pallas_call | solution.py:70
  208.3 101.0 %reduce-scatter.2.cloned.1.call-done = bf16[64,7168]{1,0:T(8,128)(2,1)} async-done(((bf16[1024,7168]{1,0:T(8,128)(2,1)}), bf16[64,7168]{1,0:T(8,128)(2,1)}) %reduce-scatter.2.cloned.1.call-update) | async-done | bytes 917520 | tf_op jit(solution)/shard_map/reduce_scatter | solution.py:152
  309.2 4.4 %all-to-all-start.1 = ((bf16[8,8,7168]{2,1,0:T(8,128)(2,1)}), bf16[8,8,7168]{2,1,0:T(8,128)(2,1)S(1)}, u32[]{:S(2)}, u32[]{:S(2)}) async-start(bf16[8,8,7168]{2,1,0:T(8,128)(2,1)} %bitcast.25), calls=%async_computation.2 | async-start | bytes 1835008 | tf_op jit(solution)/shard_map/all_to_all | solution.py:154
  314.0 0.2 select_reduce_fusion.1
  314.4 0.2 select_reduce_fusion
  314.6 13.6 %all-to-all-done.1 = bf16[8,8,7168]{2,1,0:T(8,128)(2,1)S(1)} async-done(((bf16[8,8,7168]{2,1,0:T(8,128)(2,1)}), bf16[8,8,7168]{2,1,0:T(8,128)(2,1)S(1)}, u32[]{:S(2)}, u32[]{:S(2)}) %all-to-all-start.1) | async-done | bytes 917536 | tf_op jit(solution)/shard_map/all_to_all | solution.py:154
  328.2 0.5 fusion
  328.8 0.4 convolution_convert_fusion
  329.1 0.9 all_to_all.16
  330.1 4.6 %all-to-all-start.2 = ((bf16[16,2,7168]{2,1,0:T(2,128)(2,1)}), bf16[16,2,7168]{2,1,0:T(2,128)(2,1)S(1)}, u32[]{:S(2)}, u32[]{:S(2)}) async-start(bf16[16,2,7168]{2,1,0:T(2,128)(2,1)} %all_to_all.16), calls=%async_computation.3 | async-start | bytes 917504 | tf_op jit(solution)/shard_map/all_to_all | solution.py:174
  334.7 10.6 %all-to-all-done.2 = bf16[16,2,7168]{2,1,0:T(2,128)(2,1)S(1)} async-done(((bf16[16,2,7168]{2,1,0:T(2,128)(2,1)}), bf16[16,2,7168]{2,1,0:T(2,128)(2,1)S(1)}, u32[]{:S(2)}, u32[]{:S(2)}) %all-to-all-start.2) | async-done | bytes 458784 | tf_op jit(solution)/shard_map/all_to_all | solution.py:174
  345.3 0.9 all_to_all.18
  346.2 4.7 %copy.45 = bf16[32,2,64,512]{3,2,1,0:T(8,128)(2,1)} copy(bf16[32,2,64,512]{3,2,1,0:T(8,128)(2,1)} %all-to-all-done) | data formatting | bytes 8388608
  (32 shorter events, 1.1 us)
Async XLA Ops:
  7.2 9.3 %copy-start = (bf16[32,64,512]{2,1,0:T(8,128)(2,1)S(1)}, bf16[32,64,512]{2,1,0:T(8,128)(2,1)}, u32[]{:S(2)}) copy-start(bf16[32,64,512]{2,1,0:T(8,128)(2,1)} %param.16) | copy-start | bytes 6291460
  7.2 147.2 %all-gather.2.cloned.1.call-start = ((), (), s32[]{:S(2)}) async-start(), calls=%async_computation.4 | async-start | bytes 30117888 | tf_op jit(solution)/shard_map/all_gather | solution.py:117
  23.5 79.0 %all-to-all-start = ((bf16[32,2,64,512]{3,2,1,0:T(8,128)(2,1)}), bf16[32,2,64,512]{3,2,1,0:T(8,128)(2,1)}, u32[]{:S(2)}, u32[]{:S(2)}) async-start(bf16[32,2,64,512]{3,2,1,0:T(8,128)(2,1)} %broadcast_select_fusion), calls=%async_computation | async-start | bytes 8388608 | tf_op jit(solution)/shard_map/all_to_all | solution.py:138
  30.7 278.5 %reduce-scatter.2.cloned.1.call-start = ((), (), s32[]{:S(2)}) async-start(), calls=%async_computation.5 | async-start | bytes 15597568 | tf_op jit(solution)/shard_map/reduce_scatter | solution.py:152
  208.2 105.4 %copy-start.3 = (s32[16,3]{0,1:T(4,128)S(1)}, s32[16,3]{0,1:T(4,128)}, u32[]{:S(2)}) copy-start(s32[16,3]{0,1:T(4,128)} %param.12) | copy-start | bytes 580
  208.2 106.0 %copy-start.4 = (f32[16,3]{0,1:T(4,128)S(1)}, f32[16,3]{0,1:T(4,128)}, u32[]{:S(2)}) copy-start(f32[16,3]{0,1:T(4,128)} %param.13) | copy-start | bytes 580
  208.2 120.0 %copy-start.2 = (bf16[16,7168]{1,0:T(8,128)(2,1)S(1)}, bf16[16,7168]{1,0:T(8,128)(2,1)}, u32[]{:S(2)}) copy-start(bf16[16,7168]{1,0:T(8,128)(2,1)} %param.10) | copy-start | bytes 688132
  309.2 19.0 %all-to-all-start.1 = ((bf16[8,8,7168]{2,1,0:T(8,128)(2,1)}), bf16[8,8,7168]{2,1,0:T(8,128)(2,1)S(1)}, u32[]{:S(2)}, u32[]{:S(2)}) async-start(bf16[8,8,7168]{2,1,0:T(8,128)(2,1)} %bitcast.25), calls=%async_computation.2 | async-start | bytes 1835008 | tf_op jit(solution)/shard_map/all_to_all | solution.py:154
  330.1 15.2 %all-to-all-start.2 = ((bf16[16,2,7168]{2,1,0:T(2,128)(2,1)}), bf16[16,2,7168]{2,1,0:T(2,128)(2,1)S(1)}, u32[]{:S(2)}, u32[]{:S(2)}) async-start(bf16[16,2,7168]{2,1,0:T(2,128)(2,1)} %all_to_all.16), calls=%async_computation.3 | async-start | bytes 917504 | tf_op jit(solution)/shard_map/all_to_all | solution.py:174
  345.3 5.6 %copy-start.1 = (bf16[32,64,512]{2,1,0:T(8,128)(2,1)S(1)}, bf16[32,64,512]{2,1,0:T(8,128)(2,1)}, u32[]{:S(2)}) copy-start(bf16[32,64,512]{2,1,0:T(8,128)(2,1)} %param.16) | copy-start | bytes 6291460
Sparse Core Ops, SparseCore 0:
  11.6 142.7 all-gather.1
  208.4 100.8 reduce-scatter.1

commit v2 on v1

--- a/solution.py
+++ b/solution.py
@@ -13,25 +13,27 @@
 MIB = 1 << 20
 
 
-def expert_kernel(width, hidden_dev, req_dev, cap, member_ref, rows_ref, win_ref, wout_ref, out_ref, acc_ref):
+def expert_kernel(
+    width, hidden_dev, req_dev, cap, chunk, parts, member_ref, rows_ref, win_hbm, wout_hbm, out_ref, acc_ref, pick_ref, win_ref, wout_ref, sems
+):
     rows = rows_ref.shape[0]
     slots = out_ref.shape[0]
-    chunk = 1024
-    acc_ref[...] = jnp.zeros_like(acc_ref)
-
-    def up(step, carry):
+    count = width // chunk
+    at_start = pl.program_id(0) == 0
+
+    def win_copy(step):
         cols = pl.ds(pl.multiple_of(step * chunk, chunk), chunk)
-        acc_ref[...] += lax.dot_general(
-            rows_ref[:, cols],
-            win_ref[:, cols],
-            (((1,), (1,)), ((), ())),
-            preferred_element_type=jnp.float32,
-        )
-        return carry
-
-    lax.fori_loop(0, width // chunk, up, 0)
-    gate = acc_ref[:, :hidden_dev]
-    act = (gate / (1.0 + jnp.exp(-gate)) * acc_ref[:, hidden_dev : 2 * hidden_dev]).astype(jnp.bfloat16)
+        return pltpu.make_async_copy(win_hbm.at[:, cols], win_ref.at[:, cols], sems.at[step])
+
+    def wout_copy():
+        return pltpu.make_async_copy(wout_hbm, wout_ref, sems.at[count])
+
+    @pl.when(at_start)
+    def _():
+        for step in range(count):
+            win_copy(step).start()
+        wout_copy().start()
+
     ids = rows_ref[:, width : width + ID_LANES].astype(jnp.float32)
     member = member_ref[0].astype(jnp.float32)
     hit = jnp.max(jnp.where(ids == member, 1.0, 0.0), axis=1, keepdims=True)
@@ -46,44 +48,80 @@
     block = lax.broadcasted_iota(jnp.int32, (rows, 1), 0) // req_dev
     place = jnp.where(hit > 0.0, block * cap + rank.astype(jnp.int32), -1)
     chosen = jnp.where(place == lax.broadcasted_iota(jnp.int32, (rows, slots), 1), 1.0, 0.0)
-    picked = jnp.dot(
-        jnp.transpose(chosen).astype(jnp.bfloat16), act, preferred_element_type=jnp.float32
-    ).astype(jnp.bfloat16)
+    pick_ref[...] = jnp.transpose(chosen).astype(jnp.bfloat16)
+    acc_ref[...] = jnp.zeros_like(acc_ref)
+    part_rows, part_slots = rows // parts, slots // parts
+
+    def up(step, carry):
+        cols = pl.ds(pl.multiple_of(step * chunk, chunk), chunk)
+
+        @pl.when(at_start)
+        def _():
+            win_copy(step).wait()
+
+        picked = [
+            jnp.dot(
+                pick_ref[i * part_slots : (i + 1) * part_slots, i * part_rows : (i + 1) * part_rows],
+                rows_ref[i * part_rows : (i + 1) * part_rows, cols],
+                preferred_element_type=jnp.float32,
+            ).astype(jnp.bfloat16)
+            for i in range(parts)
+        ]
+        acc_ref[...] += lax.dot_general(
+            jnp.concatenate(picked, axis=0),
+            win_ref[:, cols],
+            (((1,), (1,)), ((), ())),
+            preferred_element_type=jnp.float32,
+        )
+        return carry
+
+    lax.fori_loop(0, count, up, 0, unroll=count)
+    gate = acc_ref[:, :hidden_dev]
+    act = (gate / (1.0 + jnp.exp(-gate)) * acc_ref[:, hidden_dev : 2 * hidden_dev]).astype(jnp.bfloat16)
+
+    @pl.when(at_start)
+    def _():
+        wout_copy().wait()
 
     def down(step, carry):
         cols = pl.ds(pl.multiple_of(step * chunk, chunk), chunk)
         out_ref[:, cols] = jnp.dot(
-            picked, wout_ref[:, cols], preferred_element_type=jnp.float32
+            act, wout_ref[:, cols], preferred_element_type=jnp.float32
         ).astype(out_ref.dtype)
         return carry
 
-    lax.fori_loop(0, width // chunk, down, 0)
+    lax.fori_loop(0, count, down, 0, unroll=count)
 
 
 def run_experts(member, rows, weight_in, weight_out, req_dev, cap, devices):
     width = weight_in.shape[1]
     hidden_dev = weight_out.shape[0]
-    steps = 4
+    steps, parts, chunk = 4, 2, width // 4
     block = rows.shape[0] // steps
     slots = devices * cap // steps
-    once = pl.Buffered(1)
     return pl.pallas_call(
-        functools.partial(expert_kernel, width, hidden_dev, req_dev, cap),
+        functools.partial(expert_kernel, width, hidden_dev, req_dev, cap, chunk, parts),
         out_shape=jax.ShapeDtypeStruct((devices * cap, width), jnp.bfloat16),
         grid=(steps,),
         in_specs=[
             pl.BlockSpec(memory_space=pltpu.SMEM),
             pl.BlockSpec((block, rows.shape[1]), lambda s: (s, 0)),
-            pl.BlockSpec(weight_in.shape, lambda s: (0, 0), pipeline_mode=once),
-            pl.BlockSpec(weight_out.shape, lambda s: (0, 0), pipeline_mode=once),
+            pl.BlockSpec(memory_space=pl.ANY),
+            pl.BlockSpec(memory_space=pl.ANY),
         ],
         out_specs=pl.BlockSpec((slots, width), lambda s: (s, 0)),
-        scratch_shapes=[pltpu.VMEM((block, 2 * hidden_dev), jnp.float32)],
+        scratch_shapes=[
+            pltpu.VMEM((slots, 2 * hidden_dev), jnp.float32),
+            pltpu.VMEM((slots, block), jnp.bfloat16),
+            pltpu.VMEM(weight_in.shape, weight_in.dtype),
+            pltpu.VMEM(weight_out.shape, weight_out.dtype),
+            pltpu.SemaphoreType.DMA((width // chunk + 1,)),
+        ],
         compiler_params=pltpu.CompilerParams(vmem_limit_bytes=56 * MIB),
         cost_estimate=pl.CostEstimate(
-            flops=2 * rows.shape[0] * width * 2 * hidden_dev + 2 * devices * cap * width * hidden_dev,
+            flops=2 * devices * cap * width * (3 * hidden_dev + 2 * req_dev * 8),
             bytes_accessed=2 * (rows.size + weight_in.size + weight_out.size + devices * cap * width),
-            transcendentals=rows.shape[0] * hidden_dev,
+            transcendentals=devices * cap * hidden_dev,
         ),
     )(member, rows, weight_in, weight_out)
 
@@ -135,9 +173,11 @@
     )
     kept_mask = (positions[None, :, :] < req_len[sources][:, None, None]) & occupied[:, None, None]
     outgoing_pages = jnp.where(kept_mask[..., None], page_rows, jnp.zeros_like(page_rows))
-    moved_pages = lax.all_to_all(outgoing_pages, "attn", split_axis=0, concat_axis=0, tiled=True)
-
-    gathered, moved_pages = lax.optimization_barrier((gathered, moved_pages))
+    first_pages = lax.all_to_all(outgoing_pages[:, 0], "attn", split_axis=0, concat_axis=0, tiled=True)
+    gathered, first_pages, second_out = lax.optimization_barrier(
+        (gathered, first_pages, outgoing_pages[:, 1])
+    )
+    second_pages = lax.all_to_all(second_out, "attn", split_axis=0, concat_axis=0, tiled=True)
     member = lax.axis_index("ffn").astype(jnp.int32).reshape(1)
     hidden_dev = expert_in.shape[2]
     partial = run_experts(
@@ -149,6 +189,8 @@
         expert_cap,
         members * instances,
     )
+    moved_pages = jnp.stack([first_pages, second_pages], axis=1)
+    partial, moved_pages = lax.optimization_barrier((partial, moved_pages))
     summed = lax.psum_scatter(partial, "attn", scatter_dimension=0, tiled=True)
     results = summed.reshape(members, expert_cap, width)
     returned = lax.all_to_all(results, "ffn", split_axis=0, concat_axis=0, tiled=True)

time: 358 us -> 322 us (0.90)
  waiting for transfers between devices: 249 us -> 184 us
  blocking collectives: 0 us -> 37.4 us
  Pallas kernels: 53.8 us -> 41.3 us
    all_to_all x1, waiting for transfers between devices: 71.8 us -> 0.01 us  [body(): lax.all_to_all(second_out, 'attn', split_axis=0, concat_axis=0, tiled=True)]
    all_to_all x0 -> x1, blocking collectives: none -> 37.4 us  [body(): lax.all_to_all(outgoing_pages[:, 0], 'attn', split_axis=0, concat_axis=0,...]
    pallas_call x1, Pallas kernels: 53.8 us -> 41.3 us  [run_experts(): pl.pallas_call(functools.partial(expert_kernel, width, hidden_dev, req_de...]
    all_gather x1, waiting for transfers between devices: 51.8 us -> 63.1 us  [body(): gathered = lax.all_gather(payload, ('attn', 'ffn'), axis=0, tiled=True)]
    all_to_all x1, waiting for transfers between devices: 10.6 us -> 5.73 us  [body(): lax.all_to_all(rows_out, 'attn', split_axis=0, concat_axis=0, tiled=True)]
    another operation x1 -> x2, other arithmetic: 0.69 us -> 4.59 us  [the longest x1 3.9 us: body(): moved_pages = jnp.stack([first_pages, second_pages], axis=1)]
  transfers between devices with their start and end apart: 5 -> 5, of which waited for: 5 -> 4; matrix products, arithmetic and copies ran while one was open for 4% -> 6% of each run, Pallas kernels for 0% -> 13%
where the time goes in v2:
time: 322 us; the launch traced here: 321 us
  waiting for transfers between devices  184 us (57%)
  Pallas kernels  41.3 us (13%)
  blocking collectives  37.4 us (12%)
  starting transfers between devices  15.9 us (5%)
  local copies, waits for them, and re-layouts  14.7 us (5%)
  between operations  14.2 us (4%)
  other arithmetic  13.4 us (4%)
    reduce_scatter x1, waiting for transfers between devices, body(): summed = lax.psum_scatter(partial, 'attn', scatter_dimension=0, tiled=True)  101 us
    all_gather x1, waiting for transfers between devices, body(): gathered = lax.all_gather(payload, ('attn', 'ffn'), axis=0, tiled=True)  63.1 us
    pallas_call x1, Pallas kernels, run_experts(): pl.pallas_call(functools.partial(expert_kernel, width, hidden_dev, req_de...  41.3 us
    all_to_all x1, blocking collectives, body(): lax.all_to_all(outgoing_pages[:, 0], 'attn', split_axis=0, concat_axis=0,...  37.4 us
    all_to_all x1, waiting for transfers between devices, body(): lax.all_to_all(results, 'ffn', split_axis=0, concat_axis=0, tiled=True)  13.6 us
    all_to_all x1, starting transfers between devices, body(): lax.all_to_all(second_out, 'attn', split_axis=0, concat_axis=0, tiled=True)  6.82 us
  transfers between devices with their start and end apart: 5, of which 4 were waited for; matrix products, arithmetic and copies ran while one was open for 6% of the time, Pallas kernels for 13%

profile of v2, /device:TPU:0, one launch (start us, length us, event | category | flops | bytes accessed | tf_op | source)
XLA Modules:
  0.0 321.5 jit_solution(17780412226680929316)
XLA Ops:
  7.2 1.2 fusion.4
  8.5 0.7 convert.4
  9.3 1.1 fusion.6
  10.3 0.7 fusion.7
  11.1 0.8 copy.36
  11.8 0.7 fusion.9
  12.6 0.8 select_reduce_fusion.3
  13.4 0.7 multiply_add_fusion.1
  14.2 1.4 gather_fusion
  15.6 0.6 gather_fusion.1
  16.3 0.1 reshape.138
  16.5 2.8 gather_fusion.2
  19.4 0.1 compare_and_fusion
  19.6 2.6 broadcast_select_fusion
  22.2 1.7 slice_bitcast_fusion
  23.9 37.4 %all_to_all.27 = bf16[32,64,512]{2,1,0:T(8,128)(2,1)S(1)} all-to-all(bf16[32,64,512]{2,1,0:T(8,128)(2,1)S(1)} %get-tuple-element.23), channel_id=1, replica_groups=mesh['attn'=16,'ffn'=8] {'attn'}, dimensions={0} | all-to-all | bytes 4194304 | tf_op jit(solution)/shard_map/all_to_all | solution.py:176
  61.2 63.1 %all-gather.2.cloned.1.call-done.rows_ref = bf16[2048,7296]{1,0:T(8,128)(2,1)} async-done(((bf16[16,7296]{1,0:T(8,128)(2,1)}), bf16[2048,7296]{1,0:T(8,128)(2,1)}) %all-gather.2.cloned.1.call-update) | async-done | bytes 29884432 | tf_op jit(solution)/shard_map/all_gather | solution.py:155
  124.3 6.8 %all-to-all-start.1 = ((bf16[32,64,512]{2,1,0:T(8,128)(2,1)}), bf16[32,64,512]{2,1,0:T(8,128)(2,1)}, u32[]{:S(2)}, u32[]{:S(2)}) async-start(bf16[32,64,512]{2,1,0:T(8,128)(2,1)} %get-tuple-element.13), calls=%async_computation.1 | async-start | bytes 4194304 | tf_op jit(solution)/shard_map/all_to_all | solution.py:180
  131.2 41.3 %shard_map.113 = bf16[1024,7168]{1,0:T(8,128)(2,1)} custom-call(s32[1]{0:T(128)} %bitcast.1.member_ref, bf16[2048,7296]{1,0:T(8,128)(2,1)} %all-gather.2.cloned.1.call-done.rows_ref, bf16[640,7168]{1,0:T(8,128)(2,1)} %bitcast.37, bf16[320,7168]{1,0:T(8,128)(2,1)} %bitcast.38), custom_call_target="tpu_custom_call" | custom-call | flops 17850957824 | bytes 58327040 | tf_op jit(solution)/shard_map/pallas_call | solution.py:102
  172.5 3.9 %pad_maximum_fusion = bf16[32,2,64,512]{3,2,0,1:T(8,128)(2,1)} fusion(bf16[32,1,64,512]{3,2,0,1:T(8,128)(2,1)} %bitcast.12, bf16[32,1,64,512]{3,2,0,1:T(8,128)(2,1)S(1)} %bitcast.33), kind=kLoop, calls=%fused_computation.6 | loop fusion | flops 2097152 | bytes 8388608 | tf_op jit(solution)/shard_map/stack | solution.py:192
  176.4 101.2 %reduce-scatter.2.cloned.1.call-done = bf16[64,7168]{1,0:T(8,128)(2,1)} async-done(((bf16[1024,7168]{1,0:T(8,128)(2,1)}), bf16[64,7168]{1,0:T(8,128)(2,1)}) %reduce-scatter.2.cloned.1.call-update) | async-done | bytes 917520 | tf_op jit(solution)/shard_map/reduce_scatter | solution.py:194
  277.6 4.4 %all-to-all-start.2 = ((bf16[8,8,7168]{2,1,0:T(8,128)(2,1)}), bf16[8,8,7168]{2,1,0:T(8,128)(2,1)S(1)}, u32[]{:S(2)}, u32[]{:S(2)}) async-start(bf16[8,8,7168]{2,1,0:T(8,128)(2,1)} %bitcast.34), calls=%async_computation.3 | async-start | bytes 1835008 | tf_op jit(solution)/shard_map/all_to_all | solution.py:196
  282.4 0.2 select_reduce_fusion.1
  282.8 0.2 select_reduce_fusion
  283.0 13.6 %all-to-all-done.2 = bf16[8,8,7168]{2,1,0:T(8,128)(2,1)S(1)} async-done(((bf16[8,8,7168]{2,1,0:T(8,128)(2,1)}), bf16[8,8,7168]{2,1,0:T(8,128)(2,1)S(1)}, u32[]{:S(2)}, u32[]{:S(2)}) %all-to-all-start.2) | async-done | bytes 917536 | tf_op jit(solution)/shard_map/all_to_all | solution.py:196
  296.6 0.5 fusion
  297.2 0.4 convolution_convert_fusion
  297.6 0.9 all_to_all.20
  298.5 4.6 %all-to-all-start.3 = ((bf16[16,2,7168]{2,1,0:T(2,128)(2,1)}), bf16[16,2,7168]{2,1,0:T(2,128)(2,1)S(1)}, u32[]{:S(2)}, u32[]{:S(2)}) async-start(bf16[16,2,7168]{2,1,0:T(2,128)(2,1)} %all_to_all.20), calls=%async_computation.4 | async-start | bytes 917504 | tf_op jit(solution)/shard_map/all_to_all | solution.py:216
  303.1 4.8 %copy.42 = bf16[32,2,64,512]{3,2,1,0:T(8,128)(2,1)} copy(bf16[32,2,64,512]{3,2,0,1:T(8,128)(2,1)} %pad_maximum_fusion) | data formatting | bytes 8388608
  308.0 5.7 %all-to-all-done.3 = bf16[16,2,7168]{2,1,0:T(2,128)(2,1)S(1)} async-done(((bf16[16,2,7168]{2,1,0:T(2,128)(2,1)}), bf16[16,2,7168]{2,1,0:T(2,128)(2,1)S(1)}, u32[]{:S(2)}, u32[]{:S(2)}) %all-to-all-start.3) | async-done | bytes 458784 | tf_op jit(solution)/shard_map/all_to_all | solution.py:216
  313.7 0.9 all_to_all.22
  (35 shorter events, 1.2 us)
Async XLA Ops:
  7.2 9.3 %copy-start = (bf16[32,64,512]{2,1,0:T(8,128)(2,1)S(1)}, bf16[32,64,512]{2,1,0:T(8,128)(2,1)}, u32[]{:S(2)}) copy-start(bf16[32,64,512]{2,1,0:T(8,128)(2,1)} %param.16) | copy-start | bytes 6291460
  7.2 117.1 %all-gather.2.cloned.1.call-start = ((), (), s32[]{:S(2)}) async-start(), calls=%async_computation.5 | async-start | bytes 30117888 | tf_op jit(solution)/shard_map/all_gather | solution.py:155
  124.3 48.2 %all-to-all-start.1 = ((bf16[32,64,512]{2,1,0:T(8,128)(2,1)}), bf16[32,64,512]{2,1,0:T(8,128)(2,1)}, u32[]{:S(2)}, u32[]{:S(2)}) async-start(bf16[32,64,512]{2,1,0:T(8,128)(2,1)} %get-tuple-element.13), calls=%async_computation.1 | async-start | bytes 4194304 | tf_op jit(solution)/shard_map/all_to_all | solution.py:180
  131.2 146.5 %reduce-scatter.2.cloned.1.call-start = ((), (), s32[]{:S(2)}) async-start(), calls=%async_computation.6 | async-start | bytes 15597568 | tf_op jit(solution)/shard_map/reduce_scatter | solution.py:194
  176.4 105.7 %copy-start.3 = (s32[16,3]{0,1:T(4,128)S(1)}, s32[16,3]{0,1:T(4,128)}, u32[]{:S(2)}) copy-start(s32[16,3]{0,1:T(4,128)} %param.12) | copy-start | bytes 580
  176.4 106.3 %copy-start.4 = (f32[16,3]{0,1:T(4,128)S(1)}, f32[16,3]{0,1:T(4,128)}, u32[]{:S(2)}) copy-start(f32[16,3]{0,1:T(4,128)} %param.13) | copy-start | bytes 580
  176.4 120.2 %copy-start.2 = (bf16[16,7168]{1,0:T(8,128)(2,1)S(1)}, bf16[16,7168]{1,0:T(8,128)(2,1)}, u32[]{:S(2)}) copy-start(bf16[16,7168]{1,0:T(8,128)(2,1)} %param.10) | copy-start | bytes 688132
  277.6 19.0 %all-to-all-start.2 = ((bf16[8,8,7168]{2,1,0:T(8,128)(2,1)}), bf16[8,8,7168]{2,1,0:T(8,128)(2,1)S(1)}, u32[]{:S(2)}, u32[]{:S(2)}) async-start(bf16[8,8,7168]{2,1,0:T(8,128)(2,1)} %bitcast.34), calls=%async_computation.3 | async-start | bytes 1835008 | tf_op jit(solution)/shard_map/all_to_all | solution.py:196
  298.5 15.2 %all-to-all-start.3 = ((bf16[16,2,7168]{2,1,0:T(2,128)(2,1)}), bf16[16,2,7168]{2,1,0:T(2,128)(2,1)S(1)}, u32[]{:S(2)}, u32[]{:S(2)}) async-start(bf16[16,2,7168]{2,1,0:T(2,128)(2,1)} %all_to_all.20), calls=%async_computation.4 | async-start | bytes 917504 | tf_op jit(solution)/shard_map/all_to_all | solution.py:216
  303.1 11.5 %copy-start.1 = (bf16[32,64,512]{2,1,0:T(8,128)(2,1)S(1)}, bf16[32,64,512]{2,1,0:T(8,128)(2,1)}, u32[]{:S(2)}) copy-start(bf16[32,64,512]{2,1,0:T(8,128)(2,1)} %param.16) | copy-start | bytes 6291460
Sparse Core Ops, SparseCore 0:
  11.6 112.6 all-gather.1
  176.6 101.0 reduce-scatter.1

commit v3 on v0

v3 whole, which is shorter than its diff:
```python
import functools

import jax
import jax.numpy as jnp
from jax import lax
from jax.experimental import pallas as pl
from jax.experimental.pallas import tpu as pltpu
from jax.sharding import PartitionSpec as P

PAGE = 64
PAGES_REQ = 2
ID_LANES = 128
MIB = 1 << 20


def expert_kernel(
    hidden_dev, req_dev, cap, topk, up_steps,
    member_ref, lanes_ref, rows_ref, win_ref, wout_ref,
    main_ref, gated_ref,
    acc_ref, chosen_ref, pick_ref, picked_ref, act_ref,
):
    step = pl.program_id(0)
    groups, slots, rows = pick_ref.shape
    member = member_ref[0].astype(jnp.float32)

    @pl.when(step == 0)
    def _():
        first = lax.broadcasted_iota(jnp.int32, (rows, rows), 0)
        second = lax.broadcasted_iota(jnp.int32, (rows, rows), 1)
        before = jnp.where((second < first) & (second // req_dev == first // req_dev), 1.0, 0.0)
        block = lax.broadcasted_iota(jnp.int32, (rows, 1), 0) // req_dev
        slot = lax.broadcasted_iota(jnp.int32, (rows, slots), 1)
        for group in range(groups):
            lanes = lanes_ref[group * rows : (group + 1) * rows, :].astype(jnp.float32)
            lane = lax.broadcasted_iota(jnp.int32, lanes.shape, 1)
            hit = jnp.max(jnp.where((lanes == member) & (lane < topk), 1.0, 0.0), axis=1, keepdims=True)
            rank = jnp.dot(
                before.astype(jnp.bfloat16),
                jnp.broadcast_to(hit, (rows, 128)).astype(jnp.bfloat16),
                preferred_element_type=jnp.float32,
            )[:, :1]
            place = jnp.where(hit > 0.0, block * cap + rank.astype(jnp.int32), -1)
            chosen = jnp.where(place == slot, 1.0, 0.0)
            chosen_ref[group] = chosen.astype(jnp.bfloat16)
            pick_ref[group] = jnp.transpose(chosen).astype(jnp.bfloat16)
        acc_ref[...] = jnp.zeros_like(acc_ref)

    @pl.when(step < up_steps)
    def _():
        for group in range(groups):
            picked_ref[group * slots : (group + 1) * slots, :] = jnp.dot(
                pick_ref[group],
                rows_ref[group * rows : (group + 1) * rows, :],
                preferred_element_type=jnp.float32,
            ).astype(jnp.bfloat16)
        acc_ref[...] += lax.dot_general(
            picked_ref[...], win_ref[...], (((1,), (1,)), ((), ())), preferred_element_type=jnp.float32
        )

    @pl.when(step == up_steps - 1)
    def _():
        gate = acc_ref[:, :hidden_dev]
        act_ref[...] = (gate / (1.0 + jnp.exp(-gate)) * acc_ref[:, hidden_dev : 2 * hidden_dev]).astype(jnp.bfloat16)
        for group in range(groups):
            lanes = lanes_ref[group * rows : (group + 1) * rows, :].astype(jnp.float32)
            score = jnp.zeros((rows, 1), jnp.float32)
            for k in range(topk):
                high, low = (lanes[:, n * topk + k : n * topk + k + 1] for n in (1, 2))
                score = jnp.where(lanes[:, k : k + 1] == member, high + low, score)
            back = jnp.dot(
                chosen_ref[group], act_ref[group * slots : (group + 1) * slots, :], preferred_element_type=jnp.float32
            )
            gated_ref[group * rows : (group + 1) * rows, :] = (back * score).astype(jnp.bfloat16)

    @pl.when(step >= up_steps)
    def _():
        main_ref[...] = jnp.dot(
            act_ref[...], wout_ref[...], preferred_element_type=jnp.float32
        ).astype(main_ref.dtype)


def run_experts(member, rows, weight_in, weight_out, req_dev, cap, topk, main):
    width = weight_in.shape[1]
    hidden_dev = weight_out.shape[0]
    count = rows.shape[0]
    slots = count // req_dev * cap
    group = 16 * req_dev
    groups = count // group
    up, down = width // 7, 1536
    up_steps, down_steps = width // up, main // down

    def at_up(s):
        return (0, jnp.minimum(s, up_steps - 1))

    def at_down(s):
        return (0, jnp.maximum(s - up_steps, 0))

    return pl.pallas_call(
        functools.partial(expert_kernel, hidden_dev, req_dev, cap, topk, up_steps),
        out_shape=(
            jax.ShapeDtypeStruct((slots, main), jnp.bfloat16),
            jax.ShapeDtypeStruct((count, hidden_dev), jnp.bfloat16),
        ),
        grid=(up_steps + down_steps,),
        in_specs=[
            pl.BlockSpec(memory_space=pltpu.SMEM),
            pl.BlockSpec((count, ID_LANES), lambda s: (0, width // ID_LANES), pipeline_mode=pl.Buffered(1)),
            pl.BlockSpec((count, up), at_up),
            pl.BlockSpec((2 * hidden_dev, up), at_up),
            pl.BlockSpec((hidden_dev, down), at_down),
        ],
        out_specs=(
            pl.BlockSpec((slots, down), at_down),
            pl.BlockSpec((count, hidden_dev), lambda s: (0, 0)),
        ),
        scratch_shapes=[
            pltpu.VMEM((slots, 2 * hidden_dev), jnp.float32),
            pltpu.VMEM((groups, group, slots // groups), jnp.bfloat16),
            pltpu.VMEM((groups, slots // groups, group), jnp.bfloat16),
            pltpu.VMEM((slots, up), jnp.bfloat16),
            pltpu.VMEM((slots, hidden_dev), jnp.bfloat16),
        ],
        compiler_params=pltpu.CompilerParams(vmem_limit_bytes=52 * MIB),
        cost_estimate=pl.CostEstimate(
            flops=2 * slots * width * (2 * hidden_dev + group) + 2 * slots * hidden_dev * main,
            bytes_accessed=2 * (rows.size + weight_in.size + hidden_dev * main + slots * main + count * hidden_dev),
            transcendentals=slots * hidden_dev,
        ),
    )(member, rows, rows, weight_in, weight_out)


def reduce_side(gated, weight_out, req_dev):
    instances, chips = gated.shape[:2]
    cols = weight_out.shape[1]
    member = lax.axis_index("ffn")
    chip, core = member // 2, member % 2
    way = 1 - 2 * core
    ring = [(2 * z + c, 2 * ((z + 1 - 2 * c) % chips) + c) for z in range(chips) for c in range(2)]

    def part(target):
        rows = lax.dynamic_index_in_dim(gated, target, 1, keepdims=False).reshape(instances * req_dev, -1)
        return jnp.dot(rows, weight_out, preferred_element_type=jnp.float32)

    total = part((chip - way) % chips)
    for step in range(1, chips):
        arrived = lax.ppermute(total.astype(jnp.bfloat16), "ffn", ring)
        total = arrived.astype(jnp.float32) + part((chip - way * (1 + step)) % chips)
    spread = lax.all_to_all(
        total.astype(jnp.bfloat16).reshape(instances, req_dev, cols), "attn", split_axis=0, concat_axis=0, tiled=True
    )
    return jnp.sum(spread.astype(jnp.float32), axis=0)


def body(
    hidden,
    norm_gain,
    expert_ids,
    gate_scores,
    expert_in,
    expert_out,
    kv_pages,
    block_table,
    req_len,
    new_owner,
):
    req_dev = hidden.shape[0]
    width = hidden.shape[1]
    topk = expert_ids.shape[1]
    members = lax.axis_size("ffn")
    instances = lax.axis_size("attn")
    expert_cap = req_dev * topk * 4 // (members * 3)
    per_peer = 2 * req_dev // instances

    floats = hidden.astype(jnp.float32)
    scale = lax.rsqrt(jnp.mean(floats * floats, axis=-1, keepdims=True) + 1e-06)
    normed = (floats * scale * norm_gain).astype(jnp.bfloat16)
    gate_high = gate_scores.astype(jnp.bfloat16)
    gate_low = (gate_scores - gate_high.astype(jnp.float32)).astype(jnp.bfloat16)
    lanes = jnp.concatenate([expert_ids.astype(jnp.bfloat16), gate_high, gate_low], axis=1)
    lanes = jnp.pad(lanes, ((0, 0), (0, ID_LANES - 3 * topk)))
    payload = jnp.concatenate([normed, lanes], axis=1)
    payload, kv_pages = lax.optimization_barrier((payload, kv_pages))
    gathered = lax.all_gather(payload, ("attn", "ffn"), axis=0, tiled=True)

    owners = new_owner.reshape(-1)
    owner_hot = (owners[:, None] == jnp.arange(instances, dtype=jnp.int32)[None, :]).astype(
        jnp.int32
    )
    owner_rank = jnp.sum((jnp.cumsum(owner_hot, axis=0) - owner_hot) * owner_hot, axis=1)
    send_slot = owners * per_peer + owner_rank
    routing = jnp.arange(instances * per_peer, dtype=jnp.int32)[:, None] == send_slot[None, :]
    occupied = jnp.any(routing, axis=1)
    sources = jnp.sum(
        routing.astype(jnp.int32) * jnp.arange(req_dev, dtype=jnp.int32)[None, :], axis=1
    )
    tables = block_table[sources]
    page_rows = kv_pages[tables]
    positions = (
        jnp.arange(PAGES_REQ, dtype=jnp.int32)[:, None] * PAGE
        + jnp.arange(PAGE, dtype=jnp.int32)[None, :]
    )
    kept_mask = (positions[None, :, :] < req_len[sources][:, None, None]) & occupied[:, None, None]
    outgoing_pages = jnp.where(kept_mask[..., None], page_rows, jnp.zeros_like(page_rows))
    first_pages = lax.all_to_all(outgoing_pages[:, 0], "attn", split_axis=0, concat_axis=0, tiled=True)
    main = width - 2560
    swap = [(m, m ^ 1) for m in range(members)]
    weight_out = expert_out.reshape(expert_out.shape[1], width)
    side_out = weight_out[:, main:]
    side_out = jnp.concatenate([side_out, lax.ppermute(side_out, "ffn", swap)], axis=0)
    gathered, first_pages, second_out, side_out = lax.optimization_barrier(
        (gathered, first_pages, outgoing_pages[:, 1], side_out)
    )
    second_pages = lax.all_to_all(second_out, "attn", split_axis=0, concat_axis=0, tiled=True)
    member = lax.axis_index("ffn").astype(jnp.int32).reshape(1)
    hidden_dev = expert_in.shape[2]
    partial, gated = run_experts(
        member, gathered, expert_in.reshape(2 * hidden_dev, width), weight_out, req_dev, expert_cap, topk, main
    )
    partial, gated, second_pages = lax.optimization_barrier((partial, gated, second_pages))
    moved_pages = jnp.stack([first_pages, second_pages], axis=1)
    summed = lax.psum_scatter(partial, "attn", scatter_dimension=0, tiled=True)
    results = summed.reshape(members, expert_cap, main)
    returned = lax.all_to_all(results, "ffn", split_axis=0, concat_axis=0, tiled=True)

    gated = gated.reshape(instances, members // 2, 2, req_dev, hidden_dev)
    core = lax.axis_index("ffn") % 2
    own = lax.dynamic_index_in_dim(gated, core, 2, keepdims=False)
    other = lax.ppermute(lax.dynamic_index_in_dim(gated, 1 - core, 2, keepdims=False), "ffn", swap)
    side_mix = reduce_side(jnp.concatenate([own, other], axis=-1), side_out, req_dev)

    pair_ids = expert_ids.reshape(-1)
    onehot = (pair_ids[:, None] == jnp.arange(members, dtype=jnp.int32)[None, :]).astype(jnp.int32)
    rank_pos = jnp.sum((jnp.cumsum(onehot, axis=0) - onehot) * onehot, axis=1)
    slot_ids = pair_ids * expert_cap + rank_pos
    matches = jnp.arange(members * expert_cap, dtype=jnp.int32)[:, None] == slot_ids[None, :]
    matches = matches.reshape(members * expert_cap, req_dev, topk)
    combine_weights = jnp.einsum(
        "sjk,jk->js", matches.astype(jnp.float32), gate_scores, precision=lax.Precision.HIGHEST
    )
    main_mix = jnp.dot(
        combine_weights,
        returned.reshape(members * expert_cap, main).astype(jnp.float32),
        precision=lax.Precision.HIGHEST,
    )
    expert_mix = jnp.concatenate([main_mix, side_mix], axis=1)
    updated = (floats + expert_mix).astype(jnp.bfloat16)
    rows_out = jnp.dot(
        routing.astype(jnp.bfloat16), updated, preferred_element_type=jnp.float32
    ).astype(jnp.bfloat16)
    moved_rows = lax.all_to_all(rows_out, "attn", split_axis=0, concat_axis=0, tiled=True)
    return (moved_pages, moved_rows)


def solution(mesh):
    in_specs = (
        P(("attn", "ffn"), None),
        P(),
        P(("attn", "ffn"), None),
        P(("attn", "ffn"), None),
        P("ffn", None, "attn", None),
        P("ffn", "attn", None),
        P(("attn", "ffn"), None, None),
        P(("attn", "ffn"), None),
        P(("attn", "ffn")),
        P(("attn", "ffn"), None),
    )
    out_specs = (P(("attn", "ffn"), None, None, None), P(("attn", "ffn"), None))
    return jax.shard_map(body, mesh=mesh, in_specs=in_specs, out_specs=out_specs, check_vma=False)
```

time: 373 us -> 311 us (0.83)
  waiting for transfers between devices: 268 us -> 194 us
  blocking collectives: 34 us -> 0 us
  Pallas kernels: 0 us -> 32.4 us
  starting transfers between devices: 9.13 us -> 30 us
  matrix products: 28.2 us -> 8.68 us
  other arithmetic: 6.97 us -> 15.5 us
  local copies, waits for them, and re-layouts: 12.2 us -> 16.3 us
    reduce_scatter x1, waiting for transfers between devices: 99.2 us -> 0.01 us  [body(): summed = lax.psum_scatter(partial, 'attn', scatter_dimension=0, tiled=True)]
    ppermute x0 -> x5, waiting for transfers between devices: none -> 58.9 us  [the longest x3 56.4 us: reduce_side(): arrived = lax.ppermute(total.astype(jnp.bfloat16), 'ffn', ring)]
    all_gather x1, waiting for transfers between devices: 100 us -> 58.1 us  [body(): gathered = lax.all_gather(payload, ('attn', 'ffn'), axis=0, tiled=True)]
    all_to_all x2 -> x0, blocking collectives: 34 us -> none  [the longest x1 20 us: body(): lax.all_to_all(outgoing.reshape(members, expert_cap, width), 'ffn', split...]
    pallas_call x0 -> x1, Pallas kernels: none -> 32.4 us  [run_experts(): pl.pallas_call(functools.partial(expert_kernel, hidden_dev, req_dev, cap,...]
    all_to_all x1 -> x4, starting transfers between devices: 4.63 us -> 24.6 us  [the longest x1 7.12 us: body(): lax.all_to_all(outgoing_pages[:, 0], 'attn', split_axis=0, concat_axis=0,...]
    dot_general x5, matrix products: 27.8 us -> 8.29 us  [the longest x4 7.88 us: part(): return jnp.dot(rows, weight_out, preferred_element_type=jnp.float32)]
    concatenate x0 -> x4, other arithmetic: none -> 5.17 us  [the longest x1 3.85 us: body(): jnp.concatenate([side_out, lax.ppermute(side_out, 'ffn', swap)], axis=0)]
  transfers between devices with their start and end apart: 4 -> 12, of which waited for: 4 -> 10; matrix products, arithmetic and copies ran while one was open for 3% -> 10% of each run, Pallas kernels for 0% -> 10%
where the time goes in v3:
time: 311 us
  waiting for transfers between devices  194 us (62%)
  Pallas kernels  32.4 us (10%)
  starting transfers between devices  30 us (10%)
  local copies, waits for them, and re-layouts  16.3 us (5%)
  other arithmetic  15.5 us (5%)
  between operations  14.3 us (5%)
  matrix products  8.68 us (3%)
    all_gather x1, waiting for transfers between devices, body(): gathered = lax.all_gather(payload, ('attn', 'ffn'), axis=0, tiled=True)  58.1 us
    ppermute x3, waiting for transfers between devices, reduce_side(): arrived = lax.ppermute(total.astype(jnp.bfloat16), 'ffn', ring)  56.4 us
    all_to_all x1, waiting for transfers between devices, body(): lax.all_to_all(outgoing_pages[:, 0], 'attn', split_axis=0, concat_axis=0,...  36.3 us
    pallas_call x1, Pallas kernels, run_experts(): pl.pallas_call(functools.partial(expert_kernel, hidden_dev, req_dev, cap,...  32.4 us
    all_to_all x1, waiting for transfers between devices, reduce_side(): lax.all_to_all(total.astype(jnp.bfloat16).reshape(instances, req_dev, col...  23.2 us
    all_to_all x1, waiting for transfers between devices, body(): lax.all_to_all(results, 'ffn', split_axis=0, concat_axis=0, tiled=True)  10.6 us
    dot_general x4, matrix products, part(): return jnp.dot(rows, weight_out, preferred_element_type=jnp.float32)  7.88 us
    all_to_all x1, starting transfers between devices, body(): lax.all_to_all(outgoing_pages[:, 0], 'attn', split_axis=0, concat_axis=0,...  7.12 us
  transfers between devices with their start and end apart: 12, of which 10 were waited for; matrix products, arithmetic and copies ran while one was open for 10% of the time, Pallas kernels for 10%

profile of v3, /device:TPU:0, one launch (start us, length us, event | category | flops | bytes accessed | tf_op | source)
XLA Modules:
  0.0 310.7 jit_solution(4245436995457117011)
XLA Ops:
  9.7 1.1 fusion.3
  10.9 1.1 fusion.5
  12.7 2.7 slice.20
  17.5 2.8 gather_fusion.2
  20.7 2.6 broadcast_select_fusion
  23.3 2.3 slice_bitcast_fusion
  25.5 7.1 %all-to-all-start = ((bf16[32,64,512]{2,1,0:T(8,128)(2,1)}), bf16[32,64,512]{2,1,0:T(8,128)(2,1)S(1)}, u32[]{:S(2)}, u32[]{:S(2)}) async-start(bf16[32,64,512]{2,1,0:T(8,128)(2,1)} %get-tuple-element.31), calls=%async_computation | async-start | bytes 4194304 | tf_op jit(solution)/shard_map/all_to_all | solution.py:204
  32.7 3.9 %pad_maximum_fusion.1 = bf16[640,2560]{1,0:T(8,128)(2,1)} fusion(bf16[320,2560]{1,0:T(8,128)(2,1)} %collective-permute-done, bf16[320,2560]{1,0:T(8,128)(2,1)} %slice.20), kind=kLoop, calls=%fused_computation.7 | loop fusion | flops 6553600 | bytes 6553600 | tf_op jit(solution)/shard_map/concatenate | solution.py:209
  36.5 36.3 %all-to-all-done = bf16[32,64,512]{2,1,0:T(8,128)(2,1)S(1)} async-done(((bf16[32,64,512]{2,1,0:T(8,128)(2,1)}), bf16[32,64,512]{2,1,0:T(8,128)(2,1)S(1)}, u32[]{:S(2)}, u32[]{:S(2)}) %all-to-all-start) | async-done | bytes 2097184 | tf_op jit(solution)/shard_map/all_to_all | solution.py:204
  72.8 58.1 %all-gather.2.cloned.1.call-done.lanes_ref.rows_ref = bf16[2048,7296]{1,0:T(8,128)(2,1)} async-done(((bf16[16,7296]{1,0:T(8,128)(2,1)}), bf16[2048,7296]{1,0:T(8,128)(2,1)}) %all-gather.2.cloned.1.call-update) | async-done | bytes 29884432 | tf_op jit(solution)/shard_map/all_gather | solution.py:183
  130.9 6.8 %all-to-all-start.1 = ((bf16[32,64,512]{2,1,0:T(8,128)(2,1)}), bf16[32,64,512]{2,1,0:T(8,128)(2,1)}, u32[]{:S(2)}, u32[]{:S(2)}) async-start(bf16[32,64,512]{2,1,0:T(8,128)(2,1)} %get-tuple-element.19), calls=%async_computation.1 | async-start | bytes 4194304 | tf_op jit(solution)/shard_map/all_to_all | solution.py:213
  137.8 32.4 %shard_map.113 = (bf16[1024,4608]{1,0:T(8,128)(2,1)}, bf16[2048,320]{1,0:T(8,128)(2,1)S(1)}) custom-call(s32[1]{0:T(128)} %bitcast.10.member_ref, bf16[2048,7296]{1,0:T(8,128)(2,1)} %all-gather.2.cloned.1.call-done.lanes_ref.rows_ref, bf16[2048,7296]{1,0:T(8,128)(2,1)} %all-gather.2.cloned.1.call-done.lanes_ref.rows_ref, bf16[640,7168]{1,0:T(8,128)(2,1)} %bitcast.51, ...), custom_call_target="tpu_custom_call" | custom-call | flops 16173236224 | bytes 52756480 | tf_op jit(solution)/shard_map/pallas_call | solution.py:98
  170.2 1.0 all-to-all-done.1
  171.3 1.1 dynamic-slice_bitcast_fusion
  172.4 2.5 collective-permute-done.1
  175.4 3.3 %convolution_convert_fusion.1 = bf16[256,2560]{1,0:T(8,128)(2,1)S(1)} fusion(bf16[256,640]{1,0:T(8,128)(2,1)S(1)} %bitcast.59, bf16[640,2560]{1,0:T(8,128)(2,1)} %pad_maximum_fusion.1), kind=kOutput, calls=%fused_computation.6 | convolution fusion | flops 839516160 | bytes 4915200 | tf_op jit(solution)/shard_map/dot_general | solution.py:142
  179.0 18.8 %collective-permute-done.2 = bf16[256,2560]{1,0:T(8,128)(2,1)S(1)} collective-permute-done((bf16[256,2560]{1,0:T(8,128)(2,1)S(1)}, bf16[256,2560]{1,0:T(8,128)(2,1)S(1)}, u32[]{:S(2)}, u32[]{:S(2)}) %collective-permute-start.2) | collective-permute-done | bytes 1310752 | tf_op jit(solution)/shard_map/ppermute | solution.py:146
  197.8 1.2 add_convert_fusion.2
  199.0 18.8 %collective-permute-done.3 = bf16[256,2560]{1,0:T(8,128)(2,1)S(1)} collective-permute-done((bf16[256,2560]{1,0:T(8,128)(2,1)S(1)}, bf16[256,2560]{1,0:T(8,128)(2,1)S(1)}, u32[]{:S(2)}, u32[]{:S(2)}) %collective-permute-start.3) | collective-permute-done | bytes 1310752 | tf_op jit(solution)/shard_map/ppermute | solution.py:146
  217.8 1.2 add_convert_fusion.1
  219.1 18.8 %collective-permute-done.4 = bf16[256,2560]{1,0:T(8,128)(2,1)S(1)} collective-permute-done((bf16[256,2560]{1,0:T(8,128)(2,1)S(1)}, bf16[256,2560]{1,0:T(8,128)(2,1)S(1)}, u32[]{:S(2)}, u32[]{:S(2)}) %collective-permute-start.4) | collective-permute-done | bytes 1310752 | tf_op jit(solution)/shard_map/ppermute | solution.py:146
  237.9 2.2 add_convert_fusion
  240.2 6.3 %all-to-all-start.3 = ((bf16[16,16,2560]{2,1,0:T(8,128)(2,1)}), bf16[16,16,2560]{2,1,0:T(8,128)(2,1)S(1)}, u32[]{:S(2)}, u32[]{:S(2)}) async-start(bf16[16,16,2560]{2,1,0:T(8,128)(2,1)} %bitcast.22), calls=%async_computation.4 | async-start | bytes 2621440 | tf_op jit(solution)/shard_map/all_to_all | solution.py:148
  247.1 23.2 %all-to-all-done.3 = bf16[16,16,2560]{2,1,0:T(8,128)(2,1)S(1)} async-done(((bf16[16,16,2560]{2,1,0:T(8,128)(2,1)}), bf16[16,16,2560]{2,1,0:T(8,128)(2,1)S(1)}, u32[]{:S(2)}, u32[]{:S(2)}) %all-to-all-start.3) | async-done | bytes 1310752 | tf_op jit(solution)/shard_map/all_to_all | solution.py:148
  270.2 4.9 %all-to-all-start.2 = ((bf16[8,8,4608]{2,1,0:T(8,128)(2,1)}), bf16[8,8,4608]{2,1,0:T(8,128)(2,1)S(1)}, u32[]{:S(2)}, u32[]{:S(2)}) async-start(bf16[8,8,4608]{2,1,0:T(8,128)(2,1)} %bitcast.58), calls=%async_computation.3 | async-start | bytes 1179648 | tf_op jit(solution)/shard_map/all_to_all | solution.py:223
  275.5 10.6 %all-to-all-done.2 = bf16[8,8,4608]{2,1,0:T(8,128)(2,1)S(1)} async-done(((bf16[8,8,4608]{2,1,0:T(8,128)(2,1)}), bf16[8,8,4608]{2,1,0:T(8,128)(2,1)S(1)}, u32[]{:S(2)}, u32[]{:S(2)}) %all-to-all-start.2) | async-done | bytes 589856 | tf_op jit(solution)/shard_map/all_to_all | solution.py:223
  287.0 0.9 all_to_all.24
  288.0 4.4 %all-to-all-start.4 = ((bf16[16,2,7168]{2,1,0:T(2,128)(2,1)}), bf16[16,2,7168]{2,1,0:T(2,128)(2,1)S(1)}, u32[]{:S(2)}, u32[]{:S(2)}) async-start(bf16[16,2,7168]{2,1,0:T(2,128)(2,1)} %all_to_all.24), calls=%async_computation.5 | async-start | bytes 917504 | tf_op jit(solution)/shard_map/all_to_all | solution.py:250
  292.3 2.8 pad_maximum_fusion
  295.1 2.5 copy.51
  297.6 5.3 %all-to-all-done.4 = bf16[16,2,7168]{2,1,0:T(2,128)(2,1)S(1)} async-done(((bf16[16,2,7168]{2,1,0:T(2,128)(2,1)}), bf16[16,2,7168]{2,1,0:T(2,128)(2,1)S(1)}, u32[]{:S(2)}, u32[]{:S(2)}) %all-to-all-start.4) | async-done | bytes 458784 | tf_op jit(solution)/shard_map/all_to_all | solution.py:250
  302.9 0.9 all_to_all.26
  (69 shorter events, 8.5 us)
Async XLA Ops:
  7.2 10.4 %copy-start = (bf16[32,64,512]{2,1,0:T(8,128)(2,1)S(1)}, bf16[32,64,512]{2,1,0:T(8,128)(2,1)}, u32[]{:S(2)}) copy-start(bf16[32,64,512]{2,1,0:T(8,128)(2,1)} %param.16) | copy-start | bytes 6291460
  7.2 8.3 %copy-start.8 = (s32[16,2]{0,1:T(2,128)S(1)}, s32[16,2]{0,1:T(2,128)}, u32[]{:S(2)}) copy-start(s32[16,2]{0,1:T(2,128)} %param.17) | copy-start | bytes 388
  7.2 8.3 %copy-start.7 = (s32[16,1]{0,1:T(1,128)S(1)}, s32[16,1]{0,1:T(1,128)}, u32[]{:S(2)}) copy-start(s32[16,1]{0,1:T(1,128)} %param.19) | copy-start | bytes 196
  7.2 9.6 %copy-start.2 = (s32[16]{0:T(128)S(1)}, s32[16]{0:T(128)}, u32[]{:S(2)}) copy-start(s32[16]{0:T(128)} %param.18) | copy-start | bytes 196
  7.2 123.7 %all-gather.2.cloned.1.call-start = ((), (), s32[]{:S(2)}) async-start(), calls=%async_computation.6 | async-start | bytes 30117888 | tf_op jit(solution)/shard_map/all_gather | solution.py:183
  15.4 17.2 %collective-permute-start = (bf16[320,2560]{1,0:T(8,128)(2,1)}, bf16[320,2560]{1,0:T(8,128)(2,1)}, u32[]{:S(2)}, u32[]{:S(2)}) collective-permute-start(bf16[320,2560]{1,0:T(8,128)(2,1)} %slice.20), channel_id=1, source_target_pairs={{0,1},{1,0},{2,3},{3,2},{4,5},{5,4},{6,7},{7,6},{8,9},{9,8},{10,11... | collective-permute-start | bytes 4915208 | tf_op jit(solution)/shard_map/ppermute | solution.py:209
  25.5 47.3 %all-to-all-start = ((bf16[32,64,512]{2,1,0:T(8,128)(2,1)}), bf16[32,64,512]{2,1,0:T(8,128)(2,1)S(1)}, u32[]{:S(2)}, u32[]{:S(2)}) async-start(bf16[32,64,512]{2,1,0:T(8,128)(2,1)} %get-tuple-element.31), calls=%async_computation | async-start | bytes 4194304 | tf_op jit(solution)/shard_map/all_to_all | solution.py:204
  72.8 65.0 %copy-start.4 = (bf16[32,64,512]{2,1,0:T(8,128)(2,1)}, bf16[32,64,512]{2,1,0:T(8,128)(2,1)S(1)}, u32[]{:S(2)}) copy-start(bf16[32,64,512]{2,1,0:T(8,128)(2,1)S(1)} %all-to-all-done) | copy-start | bytes 6291460
  130.9 40.4 %all-to-all-start.1 = ((bf16[32,64,512]{2,1,0:T(8,128)(2,1)}), bf16[32,64,512]{2,1,0:T(8,128)(2,1)}, u32[]{:S(2)}, u32[]{:S(2)}) async-start(bf16[32,64,512]{2,1,0:T(8,128)(2,1)} %get-tuple-element.19), calls=%async_computation.1 | async-start | bytes 4194304 | tf_op jit(solution)/shard_map/all_to_all | solution.py:213
  137.7 132.5 %reduce-scatter.2.cloned.1.call-start = ((), (), s32[]{:S(2)}) async-start(), calls=%async_computation.7 | async-start | bytes 10027008 | tf_op jit(solution)/shard_map/reduce_scatter | solution.py:221
  172.4 2.5 collective-permute-start.1
  175.4 22.3 %copy-start.3 = (bf16[640,2560]{1,0:T(8,128)(2,1)S(1)}, bf16[640,2560]{1,0:T(8,128)(2,1)}, u32[]{:S(2)}) copy-start(bf16[640,2560]{1,0:T(8,128)(2,1)} %pad_maximum_fusion.1) | copy-start | bytes 9830404
  178.7 19.1 %collective-permute-start.2 = (bf16[256,2560]{1,0:T(8,128)(2,1)S(1)}, bf16[256,2560]{1,0:T(8,128)(2,1)S(1)}, u32[]{:S(2)}, u32[]{:S(2)}) collective-permute-start(bf16[256,2560]{1,0:T(8,128)(2,1)S(1)} %convolution_convert_fusion.1), channel_id=1, source_target_pairs={{0,2},{1,7},{2,4},{3,1},{4,6},{5,3},{6,0},{7,5},{8,10},{9,15},{10,... | collective-permute-start | bytes 3932168 | tf_op jit(solution)/shard_map/ppermute | solution.py:146
  199.0 18.9 %collective-permute-start.3 = (bf16[256,2560]{1,0:T(8,128)(2,1)S(1)}, bf16[256,2560]{1,0:T(8,128)(2,1)S(1)}, u32[]{:S(2)}, u32[]{:S(2)}) collective-permute-start(bf16[256,2560]{1,0:T(8,128)(2,1)S(1)} %add_convert_fusion.2), channel_id=1, source_target_pairs={{0,2},{1,7},{2,4},{3,1},{4,6},{5,3},{6,0},{7,5},{8,10},{9,15},{10,... | collective-permute-start | bytes 3932168 | tf_op jit(solution)/shard_map/ppermute | solution.py:146
  219.0 18.9 %collective-permute-start.4 = (bf16[256,2560]{1,0:T(8,128)(2,1)S(1)}, bf16[256,2560]{1,0:T(8,128)(2,1)S(1)}, u32[]{:S(2)}, u32[]{:S(2)}) collective-permute-start(bf16[256,2560]{1,0:T(8,128)(2,1)S(1)} %add_convert_fusion.1), channel_id=1, source_target_pairs={{0,2},{1,7},{2,4},{3,1},{4,6},{5,3},{6,0},{7,5},{8,10},{9,15},{10,... | collective-permute-start | bytes 3932168 | tf_op jit(solution)/shard_map/ppermute | solution.py:146
  240.2 6.3 %copy-start.6 = (s32[16,3]{0,1:T(4,128)S(1)}, s32[16,3]{0,1:T(4,128)}, u32[]{:S(2)}) copy-start(s32[16,3]{0,1:T(4,128)} %param.12) | copy-start | bytes 580
  240.2 46.4 %copy-start.5 = (bf16[16,7168]{1,0:T(8,128)(2,1)S(1)}, bf16[16,7168]{1,0:T(8,128)(2,1)}, u32[]{:S(2)}) copy-start(bf16[16,7168]{1,0:T(8,128)(2,1)} %param.10) | copy-start | bytes 688132
  240.2 30.0 %all-to-all-start.3 = ((bf16[16,16,2560]{2,1,0:T(8,128)(2,1)}), bf16[16,16,2560]{2,1,0:T(8,128)(2,1)S(1)}, u32[]{:S(2)}, u32[]{:S(2)}) async-start(bf16[16,16,2560]{2,1,0:T(8,128)(2,1)} %bitcast.22), calls=%async_computation.4 | async-start | bytes 2621440 | tf_op jit(solution)/shard_map/all_to_all | solution.py:148
  270.2 16.0 %all-to-all-start.2 = ((bf16[8,8,4608]{2,1,0:T(8,128)(2,1)}), bf16[8,8,4608]{2,1,0:T(8,128)(2,1)S(1)}, u32[]{:S(2)}, u32[]{:S(2)}) async-start(bf16[8,8,4608]{2,1,0:T(8,128)(2,1)} %bitcast.58), calls=%async_computation.3 | async-start | bytes 1179648 | tf_op jit(solution)/shard_map/all_to_all | solution.py:223
  288.0 15.0 %all-to-all-start.4 = ((bf16[16,2,7168]{2,1,0:T(2,128)(2,1)}), bf16[16,2,7168]{2,1,0:T(2,128)(2,1)S(1)}, u32[]{:S(2)}, u32[]{:S(2)}) async-start(bf16[16,2,7168]{2,1,0:T(2,128)(2,1)} %all_to_all.24), calls=%async_computation.5 | async-start | bytes 917504 | tf_op jit(solution)/shard_map/all_to_all | solution.py:250
  292.3 11.5 %copy-start.1 = (bf16[32,64,512]{2,1,0:T(8,128)(2,1)S(1)}, bf16[32,64,512]{2,1,0:T(8,128)(2,1)}, u32[]{:S(2)}) copy-start(bf16[32,64,512]{2,1,0:T(8,128)(2,1)} %param.16) | copy-start | bytes 6291460
Sparse Core Ops, SparseCore 0:
  12.9 118.0 all-gather.1
  171.4 97.4 reduce-scatter.1

commit v4 on v3

--- a/solution.py
+++ b/solution.py
@@ -11,6 +11,29 @@
 PAGES_REQ = 2
 ID_LANES = 128
 MIB = 1 << 20
+
+
+def payload_kernel(width, hidden_ref, gain_ref, ids_ref, gates_ref, out_ref, table_ref):
+    floats = hidden_ref[...].astype(jnp.float32)
+    scale = lax.rsqrt(jnp.mean(floats * floats, axis=-1, keepdims=True) + 1e-06)
+    out_ref[:, :width] = (floats * scale * gain_ref[...]).astype(out_ref.dtype)
+    topk, rows = ids_ref.shape
+    gates = gates_ref[...]
+    high = gates.astype(jnp.bfloat16).astype(jnp.float32)
+    table_ref[...] = jnp.zeros_like(table_ref)
+    for n, part in enumerate((ids_ref[...].astype(jnp.float32), high, gates - high)):
+        table_ref[n * topk : (n + 1) * topk, :rows] = part
+    out_ref[:, width:] = jnp.transpose(table_ref[...])[:rows, :].astype(out_ref.dtype)
+
+
+def make_payload(hidden, gain, ids, gates):
+    rows, width = hidden.shape
+    return pl.pallas_call(
+        functools.partial(payload_kernel, width),
+        out_shape=jax.ShapeDtypeStruct((rows, width + ID_LANES), jnp.bfloat16),
+        scratch_shapes=[pltpu.VMEM((ID_LANES, ID_LANES), jnp.float32)],
+        compiler_params=pltpu.CompilerParams(vmem_limit_bytes=60 * MIB),
+    )(hidden, gain.reshape(1, width), ids.T, gates.T)
 
 
 def expert_kernel(
@@ -137,16 +160,20 @@
     way = 1 - 2 * core
     ring = [(2 * z + c, 2 * ((z + 1 - 2 * c) % chips) + c) for z in range(chips) for c in range(2)]
 
-    def part(target):
+    def part(target, span):
         rows = lax.dynamic_index_in_dim(gated, target, 1, keepdims=False).reshape(instances * req_dev, -1)
-        return jnp.dot(rows, weight_out, preferred_element_type=jnp.float32)
-
-    total = part((chip - way) % chips)
-    for step in range(1, chips):
-        arrived = lax.ppermute(total.astype(jnp.bfloat16), "ffn", ring)
-        total = arrived.astype(jnp.float32) + part((chip - way * (1 + step)) % chips)
+        return jnp.dot(rows, weight_out[:, span], preferred_element_type=jnp.float32)
+
+    def ring_sum(span):
+        total = part((chip - way) % chips, span)
+        for step in range(1, chips):
+            arrived = lax.ppermute(total.astype(jnp.bfloat16), "ffn", ring)
+            total = arrived.astype(jnp.float32) + part((chip - way * (1 + step)) % chips, span)
+        return total.astype(jnp.bfloat16)
+
+    total = jnp.concatenate([ring_sum(slice(0, cols // 2)), ring_sum(slice(cols // 2, cols))], axis=1)
     spread = lax.all_to_all(
-        total.astype(jnp.bfloat16).reshape(instances, req_dev, cols), "attn", split_axis=0, concat_axis=0, tiled=True
+        total.reshape(instances, req_dev, cols), "attn", split_axis=0, concat_axis=0, tiled=True
     )
     return jnp.sum(spread.astype(jnp.float32), axis=0)
 
@@ -172,13 +199,7 @@
     per_peer = 2 * req_dev // instances
 
     floats = hidden.astype(jnp.float32)
-    scale = lax.rsqrt(jnp.mean(floats * floats, axis=-1, keepdims=True) + 1e-06)
-    normed = (floats * scale * norm_gain).astype(jnp.bfloat16)
-    gate_high = gate_scores.astype(jnp.bfloat16)
-    gate_low = (gate_scores - gate_high.astype(jnp.float32)).astype(jnp.bfloat16)
-    lanes = jnp.concatenate([expert_ids.astype(jnp.bfloat16), gate_high, gate_low], axis=1)
-    lanes = jnp.pad(lanes, ((0, 0), (0, ID_LANES - 3 * topk)))
-    payload = jnp.concatenate([normed, lanes], axis=1)
+    payload = make_payload(hidden, norm_gain, expert_ids, gate_scores)
     payload, kv_pages = lax.optimization_barrier((payload, kv_pages))
     gathered = lax.all_gather(payload, ("attn", "ffn"), axis=0, tiled=True)
 

time: 311 us -> 304 us (0.977)
  waiting for transfers between devices: 194 us -> 188 us
  other arithmetic: 15.5 us -> 11.6 us
    ppermute x3 -> x6, waiting for transfers between devices: 56.4 us -> 40.8 us  [ring_sum(): arrived = lax.ppermute(total.astype(jnp.bfloat16), 'ffn', ring)]
    reduce_scatter x1, waiting for transfers between devices: 0.01 us -> 10 us  [body(): summed = lax.psum_scatter(partial, 'attn', scatter_dimension=0, tiled=True)]
    all_gather x1, waiting for transfers between devices: 58.1 us -> 66.2 us  [body(): gathered = lax.all_gather(payload, ('attn', 'ffn'), axis=0, tiled=True)]
    all_to_all x1, waiting for transfers between devices: 36.3 us -> 31.8 us  [body(): lax.all_to_all(outgoing_pages[:, 0], 'attn', split_axis=0, concat_axis=0,...]
    all_to_all x1, waiting for transfers between devices: 23.2 us -> 18.9 us  [reduce_side(): lax.all_to_all(total.reshape(instances, req_dev, cols), 'attn', split_axi...]
    dot_general x4 -> x8, matrix products: 7.88 us -> 7.26 us  [part(): jnp.dot(rows, weight_out[:, span], preferred_element_type=jnp.float32)]
  transfers between devices with their start and end apart: 12 -> 15, of which waited for: 10 -> 14; matrix products, arithmetic and copies ran while one was open for 10% -> 11% of each run, Pallas kernels for 10% -> 11%
where the time goes in v4:
time: 304 us; the launch traced here: 303 us
  waiting for transfers between devices  188 us (62%)
  Pallas kernels  34.3 us (11%)
  starting transfers between devices  31.3 us (10%)
  local copies, waits for them, and re-layouts  15.3 us (5%)
  between operations  14.4 us (5%)
  other arithmetic  11.6 us (4%)
  matrix products  8.06 us (3%)
    all_gather x1, waiting for transfers between devices, body(): gathered = lax.all_gather(payload, ('attn', 'ffn'), axis=0, tiled=True)  66.2 us
    ppermute x6, waiting for transfers between devices, ring_sum(): arrived = lax.ppermute(total.astype(jnp.bfloat16), 'ffn', ring)  40.8 us
    pallas_call x1, Pallas kernels, run_experts(): pl.pallas_call(functools.partial(expert_kernel, hidden_dev, req_dev, cap,...  32.3 us
    all_to_all x1, waiting for transfers between devices, body(): lax.all_to_all(outgoing_pages[:, 0], 'attn', split_axis=0, concat_axis=0,...  31.8 us
    all_to_all x1, waiting for transfers between devices, reduce_side(): lax.all_to_all(total.reshape(instances, req_dev, cols), 'attn', split_axi...  18.9 us
    all_to_all x1, waiting for transfers between devices, body(): lax.all_to_all(results, 'ffn', split_axis=0, concat_axis=0, tiled=True)  10.6 us
    reduce_scatter x1, waiting for transfers between devices, body(): summed = lax.psum_scatter(partial, 'attn', scatter_dimension=0, tiled=True)  10 us
    dot_general x8, matrix products, part(): jnp.dot(rows, weight_out[:, span], preferred_element_type=jnp.float32)  7.26 us
  transfers between devices with their start and end apart: 15, of which 14 were waited for; matrix products, arithmetic and copies ran while one was open for 11% of the time, Pallas kernels for 11%

profile of v4, /device:TPU:0, one launch (start us, length us, event | category | flops | bytes accessed | tf_op | source)
XLA Modules:
  0.0 303.0 jit_solution(12774530666312094478)
XLA Ops:
  7.3 2.0 shard_map.113
  9.3 2.7 slice.34
  14.1 2.8 gather_fusion.2
  17.2 2.6 broadcast_select_fusion
  19.8 2.2 slice_bitcast_fusion
  22.0 7.1 %all-to-all-start = ((bf16[32,64,512]{2,1,0:T(8,128)(2,1)}), bf16[32,64,512]{2,1,0:T(8,128)(2,1)S(1)}, u32[]{:S(2)}, u32[]{:S(2)}) async-start(bf16[32,64,512]{2,1,0:T(8,128)(2,1)} %get-tuple-element.29), calls=%async_computation | async-start | bytes 4194304 | tf_op jit(solution)/shard_map/all_to_all | solution.py:225
  29.2 3.9 %pad_maximum_fusion.1 = bf16[640,2560]{1,0:T(8,128)(2,1)} fusion(bf16[320,2560]{1,0:T(8,128)(2,1)} %collective-permute-done, bf16[320,2560]{1,0:T(8,128)(2,1)} %slice.34), kind=kLoop, calls=%fused_computation.6 | loop fusion | flops 6553600 | bytes 6553600 | tf_op jit(solution)/shard_map/concatenate | solution.py:230
  33.1 31.8 %all-to-all-done = bf16[32,64,512]{2,1,0:T(8,128)(2,1)S(1)} async-done(((bf16[32,64,512]{2,1,0:T(8,128)(2,1)}), bf16[32,64,512]{2,1,0:T(8,128)(2,1)S(1)}, u32[]{:S(2)}, u32[]{:S(2)}) %all-to-all-start) | async-done | bytes 2097184 | tf_op jit(solution)/shard_map/all_to_all | solution.py:225
  64.8 66.2 %all-gather.2.cloned.1.call-done.lanes_ref.rows_ref = bf16[2048,7296]{1,0:T(8,128)(2,1)} async-done(((bf16[16,7296]{1,0:T(8,128)(2,1)}), bf16[2048,7296]{1,0:T(8,128)(2,1)}) %all-gather.2.cloned.1.call-update) | async-done | bytes 29884432 | tf_op jit(solution)/shard_map/all_gather | solution.py:204
  131.0 6.8 %all-to-all-start.1 = ((bf16[32,64,512]{2,1,0:T(8,128)(2,1)}), bf16[32,64,512]{2,1,0:T(8,128)(2,1)}, u32[]{:S(2)}, u32[]{:S(2)}) async-start(bf16[32,64,512]{2,1,0:T(8,128)(2,1)} %get-tuple-element.19), calls=%async_computation.1 | async-start | bytes 4194304 | tf_op jit(solution)/shard_map/all_to_all | solution.py:234
  137.9 32.3 %shard_map.114 = (bf16[1024,4608]{1,0:T(8,128)(2,1)}, bf16[2048,320]{1,0:T(8,128)(2,1)S(1)}) custom-call(s32[1]{0:T(128)} %bitcast.13.member_ref, bf16[2048,7296]{1,0:T(8,128)(2,1)} %all-gather.2.cloned.1.call-done.lanes_ref.rows_ref, bf16[2048,7296]{1,0:T(8,128)(2,1)} %all-gather.2.cloned.1.call-done.lanes_ref.rows_ref, bf16[640,7168]{1,0:T(8,128)(2,1)} %bitcast.54, ...), custom_call_target="tpu_custom_call" | custom-call | flops 16173236224 | bytes 52756480 | tf_op jit(solution)/shard_map/pallas_call | solution.py:121
  170.2 1.1 all-to-all-done.1
  171.4 1.1 dynamic-slice_bitcast_fusion
  172.5 2.5 collective-permute-done.1
  175.5 2.4 convolution_convert_fusion.1
  178.7 1.5 collective-permute-start.2
  180.2 9.6 %collective-permute-done.5 = bf16[256,1280]{1,0:T(8,128)(2,1)S(1)} collective-permute-done((bf16[256,1280]{1,0:T(8,128)(2,1)S(1)}, bf16[256,1280]{1,0:T(8,128)(2,1)S(1)}, u32[]{:S(2)}, u32[]{:S(2)}) %collective-permute-start.5) | collective-permute-done | bytes 655392 | tf_op jit(solution)/shard_map/ppermute | solution.py:170
  190.6 6.2 %collective-permute-done.2 = bf16[256,1280]{1,0:T(8,128)(2,1)S(1)} collective-permute-done((bf16[256,1280]{1,0:T(8,128)(2,1)S(1)}, bf16[256,1280]{1,0:T(8,128)(2,1)S(1)}, u32[]{:S(2)}, u32[]{:S(2)}) %collective-permute-start.2) | collective-permute-done | bytes 655392 | tf_op jit(solution)/shard_map/ppermute | solution.py:170
  197.6 6.2 %collective-permute-done.6 = bf16[256,1280]{1,0:T(8,128)(2,1)S(1)} collective-permute-done((bf16[256,1280]{1,0:T(8,128)(2,1)S(1)}, bf16[256,1280]{1,0:T(8,128)(2,1)S(1)}, u32[]{:S(2)}, u32[]{:S(2)}) %collective-permute-start.6) | collective-permute-done | bytes 655392 | tf_op jit(solution)/shard_map/ppermute | solution.py:170
  204.6 6.2 %collective-permute-done.3 = bf16[256,1280]{1,0:T(8,128)(2,1)S(1)} collective-permute-done((bf16[256,1280]{1,0:T(8,128)(2,1)S(1)}, bf16[256,1280]{1,0:T(8,128)(2,1)S(1)}, u32[]{:S(2)}, u32[]{:S(2)}) %collective-permute-start.3) | collective-permute-done | bytes 655392 | tf_op jit(solution)/shard_map/ppermute | solution.py:170
  211.6 6.2 %collective-permute-done.7 = bf16[256,1280]{1,0:T(8,128)(2,1)S(1)} collective-permute-done((bf16[256,1280]{1,0:T(8,128)(2,1)S(1)}, bf16[256,1280]{1,0:T(8,128)(2,1)S(1)}, u32[]{:S(2)}, u32[]{:S(2)}) %collective-permute-start.7) | collective-permute-done | bytes 655392 | tf_op jit(solution)/shard_map/ppermute | solution.py:170
  218.6 6.3 %collective-permute-done.4 = bf16[256,1280]{1,0:T(8,128)(2,1)S(1)} collective-permute-done((bf16[256,1280]{1,0:T(8,128)(2,1)S(1)}, bf16[256,1280]{1,0:T(8,128)(2,1)S(1)}, u32[]{:S(2)}, u32[]{:S(2)}) %collective-permute-start.4) | collective-permute-done | bytes 655392 | tf_op jit(solution)/shard_map/ppermute | solution.py:170
  225.6 1.1 pad_maximum_fusion.2
  226.8 6.0 %all-to-all-start.3 = ((bf16[16,16,2560]{2,1,0:T(8,128)(2,1)}), bf16[16,16,2560]{2,1,0:T(8,128)(2,1)S(1)}, u32[]{:S(2)}, u32[]{:S(2)}) async-start(bf16[16,16,2560]{2,1,0:T(8,128)(2,1)} %bitcast.25), calls=%async_computation.4 | async-start | bytes 2621440 | tf_op jit(solution)/shard_map/all_to_all | solution.py:175
  233.5 18.9 %all-to-all-done.3 = bf16[16,16,2560]{2,1,0:T(8,128)(2,1)S(1)} async-done(((bf16[16,16,2560]{2,1,0:T(8,128)(2,1)}), bf16[16,16,2560]{2,1,0:T(8,128)(2,1)S(1)}, u32[]{:S(2)}, u32[]{:S(2)}) %all-to-all-start.3) | async-done | bytes 1310752 | tf_op jit(solution)/shard_map/all_to_all | solution.py:175
  252.4 10.0 %reduce-scatter.2.cloned.1.call-done = bf16[64,4608]{1,0:T(8,128)(2,1)} async-done(((bf16[1024,4608]{1,0:T(8,128)(2,1)}), bf16[64,4608]{1,0:T(8,128)(2,1)}) %reduce-scatter.2.cloned.1.call-update) | async-done | bytes 589840 | tf_op jit(solution)/shard_map/reduce_scatter | solution.py:242
  262.4 4.8 %all-to-all-start.2 = ((bf16[8,8,4608]{2,1,0:T(8,128)(2,1)}), bf16[8,8,4608]{2,1,0:T(8,128)(2,1)S(1)}, u32[]{:S(2)}, u32[]{:S(2)}) async-start(bf16[8,8,4608]{2,1,0:T(8,128)(2,1)} %bitcast.58), calls=%async_computation.3 | async-start | bytes 1179648 | tf_op jit(solution)/shard_map/all_to_all | solution.py:244
  267.6 10.6 %all-to-all-done.2 = bf16[8,8,4608]{2,1,0:T(8,128)(2,1)S(1)} async-done(((bf16[8,8,4608]{2,1,0:T(8,128)(2,1)}), bf16[8,8,4608]{2,1,0:T(8,128)(2,1)S(1)}, u32[]{:S(2)}, u32[]{:S(2)}) %all-to-all-start.2) | async-done | bytes 589856 | tf_op jit(solution)/shard_map/all_to_all | solution.py:244
  280.0 4.6 %all-to-all-start.4 = ((bf16[16,2,7168]{2,1,0:T(2,128)(2,1)}), bf16[16,2,7168]{2,1,0:T(2,128)(2,1)S(1)}, u32[]{:S(2)}, u32[]{:S(2)}) async-start(bf16[16,2,7168]{2,1,0:T(2,128)(2,1)} %all_to_all.24), calls=%async_computation.5 | async-start | bytes 917504 | tf_op jit(solution)/shard_map/all_to_all | solution.py:271
  284.6 2.0 pad_maximum_fusion
  286.6 2.5 copy.31
  289.1 6.1 %all-to-all-done.4 = bf16[16,2,7168]{2,1,0:T(2,128)(2,1)S(1)} async-done(((bf16[16,2,7168]{2,1,0:T(2,128)(2,1)}), bf16[16,2,7168]{2,1,0:T(2,128)(2,1)S(1)}, u32[]{:S(2)}, u32[]{:S(2)}) %all-to-all-start.4) | async-done | bytes 458784 | tf_op jit(solution)/shard_map/all_to_all | solution.py:271
  (75 shorter events, 12.0 us)
Async XLA Ops:
  7.2 6.9 %copy-start = (bf16[32,64,512]{2,1,0:T(8,128)(2,1)S(1)}, bf16[32,64,512]{2,1,0:T(8,128)(2,1)}, u32[]{:S(2)}) copy-start(bf16[32,64,512]{2,1,0:T(8,128)(2,1)} %param.16) | copy-start | bytes 6291460
  7.2 4.8 %copy-start.10 = (s32[16,2]{0,1:T(2,128)S(1)}, s32[16,2]{0,1:T(2,128)}, u32[]{:S(2)}) copy-start(s32[16,2]{0,1:T(2,128)} %param.17) | copy-start | bytes 388
  7.2 4.9 %copy-start.9 = (s32[16,1]{0,1:T(1,128)S(1)}, s32[16,1]{0,1:T(1,128)}, u32[]{:S(2)}) copy-start(s32[16,1]{0,1:T(1,128)} %param.19) | copy-start | bytes 196
  7.2 123.8 %all-gather.2.cloned.1.call-start = ((), (), s32[]{:S(2)}) async-start(), calls=%async_computation.6 | async-start | bytes 30117888 | tf_op jit(solution)/shard_map/all_gather | solution.py:204
  7.2 6.1 %copy-start.2 = (s32[16]{0:T(128)S(1)}, s32[16]{0:T(128)}, u32[]{:S(2)}) copy-start(s32[16]{0:T(128)} %param.18) | copy-start | bytes 196
  12.0 17.2 %collective-permute-start = (bf16[320,2560]{1,0:T(8,128)(2,1)}, bf16[320,2560]{1,0:T(8,128)(2,1)}, u32[]{:S(2)}, u32[]{:S(2)}) collective-permute-start(bf16[320,2560]{1,0:T(8,128)(2,1)} %slice.34), channel_id=1, source_target_pairs={{0,1},{1,0},{2,3},{3,2},{4,5},{5,4},{6,7},{7,6},{8,9},{9,8},{10,11... | collective-permute-start | bytes 4915208 | tf_op jit(solution)/shard_map/ppermute | solution.py:230
  22.0 42.8 %all-to-all-start = ((bf16[32,64,512]{2,1,0:T(8,128)(2,1)}), bf16[32,64,512]{2,1,0:T(8,128)(2,1)S(1)}, u32[]{:S(2)}, u32[]{:S(2)}) async-start(bf16[32,64,512]{2,1,0:T(8,128)(2,1)} %get-tuple-element.29), calls=%async_computation | async-start | bytes 4194304 | tf_op jit(solution)/shard_map/all_to_all | solution.py:225
  64.8 66.2 %copy-start.3 = (bf16[32,64,512]{2,1,0:T(8,128)(2,1)}, bf16[32,64,512]{2,1,0:T(8,128)(2,1)S(1)}, u32[]{:S(2)}) copy-start(bf16[32,64,512]{2,1,0:T(8,128)(2,1)S(1)} %all-to-all-done) | copy-start | bytes 6291460
  131.0 40.4 %all-to-all-start.1 = ((bf16[32,64,512]{2,1,0:T(8,128)(2,1)}), bf16[32,64,512]{2,1,0:T(8,128)(2,1)}, u32[]{:S(2)}, u32[]{:S(2)}) async-start(bf16[32,64,512]{2,1,0:T(8,128)(2,1)} %get-tuple-element.19), calls=%async_computation.1 | async-start | bytes 4194304 | tf_op jit(solution)/shard_map/all_to_all | solution.py:234
  137.8 124.5 %reduce-scatter.2.cloned.1.call-start = ((), (), s32[]{:S(2)}) async-start(), calls=%async_computation.7 | async-start | bytes 10027008 | tf_op jit(solution)/shard_map/reduce_scatter | solution.py:242
  172.5 2.5 collective-permute-start.1
  175.0 3.0 copy-start.5
  177.9 11.9 %collective-permute-start.5 = (bf16[256,1280]{1,0:T(8,128)(2,1)S(1)}, bf16[256,1280]{1,0:T(8,128)(2,1)S(1)}, u32[]{:S(2)}, u32[]{:S(2)}) collective-permute-start(bf16[256,1280]{1,0:T(8,128)(2,1)S(1)} %convolution_convert_fusion.1), channel_id=1, source_target_pairs={{0,2},{1,7},{2,4},{3,1},{4,6},{5,3},{6,0},{7,5},{8,10},{9,15},{10,... | collective-permute-start | bytes 1966088 | tf_op jit(solution)/shard_map/ppermute | solution.py:170
  178.7 18.1 %collective-permute-start.2 = (bf16[256,1280]{1,0:T(8,128)(2,1)S(1)}, bf16[256,1280]{1,0:T(8,128)(2,1)S(1)}, u32[]{:S(2)}, u32[]{:S(2)}) collective-permute-start(bf16[256,1280]{1,0:T(8,128)(2,1)S(1)} %convolution_convert_fusion.2), channel_id=1, source_target_pairs={{0,2},{1,7},{2,4},{3,1},{4,6},{5,3},{6,0},{7,5},{8,10},{9,15},{10,... | collective-permute-start | bytes 1966088 | tf_op jit(solution)/shard_map/ppermute | solution.py:170
  190.5 13.3 %collective-permute-start.6 = (bf16[256,1280]{1,0:T(8,128)(2,1)S(1)}, bf16[256,1280]{1,0:T(8,128)(2,1)S(1)}, u32[]{:S(2)}, u32[]{:S(2)}) collective-permute-start(bf16[256,1280]{1,0:T(8,128)(2,1)S(1)} %add_convert_fusion.2), channel_id=1, source_target_pairs={{0,2},{1,7},{2,4},{3,1},{4,6},{5,3},{6,0},{7,5},{8,10},{9,15},{10,... | collective-permute-start | bytes 1966088 | tf_op jit(solution)/shard_map/ppermute | solution.py:170
  197.5 13.3 %collective-permute-start.3 = (bf16[256,1280]{1,0:T(8,128)(2,1)S(1)}, bf16[256,1280]{1,0:T(8,128)(2,1)S(1)}, u32[]{:S(2)}, u32[]{:S(2)}) collective-permute-start(bf16[256,1280]{1,0:T(8,128)(2,1)S(1)} %add_convert_fusion.5), channel_id=1, source_target_pairs={{0,2},{1,7},{2,4},{3,1},{4,6},{5,3},{6,0},{7,5},{8,10},{9,15},{10,... | collective-permute-start | bytes 1966088 | tf_op jit(solution)/shard_map/ppermute | solution.py:170
  204.5 13.3 %collective-permute-start.7 = (bf16[256,1280]{1,0:T(8,128)(2,1)S(1)}, bf16[256,1280]{1,0:T(8,128)(2,1)S(1)}, u32[]{:S(2)}, u32[]{:S(2)}) collective-permute-start(bf16[256,1280]{1,0:T(8,128)(2,1)S(1)} %add_convert_fusion.1), channel_id=1, source_target_pairs={{0,2},{1,7},{2,4},{3,1},{4,6},{5,3},{6,0},{7,5},{8,10},{9,15},{10,... | collective-permute-start | bytes 1966088 | tf_op jit(solution)/shard_map/ppermute | solution.py:170
  211.6 13.3 %collective-permute-start.4 = (bf16[256,1280]{1,0:T(8,128)(2,1)S(1)}, bf16[256,1280]{1,0:T(8,128)(2,1)S(1)}, u32[]{:S(2)}, u32[]{:S(2)}) collective-permute-start(bf16[256,1280]{1,0:T(8,128)(2,1)S(1)} %add_convert_fusion.4), channel_id=1, source_target_pairs={{0,2},{1,7},{2,4},{3,1},{4,6},{5,3},{6,0},{7,5},{8,10},{9,15},{10,... | collective-permute-start | bytes 1966088 | tf_op jit(solution)/shard_map/ppermute | solution.py:170
  225.6 7.2 %copy-start.7 = (f32[16,3]{0,1:T(4,128)S(1)}, f32[16,3]{0,1:T(4,128)}, u32[]{:S(2)}) copy-start(f32[16,3]{0,1:T(4,128)} %param.13) | copy-start | bytes 580
  225.6 7.3 %copy-start.8 = (s32[16,3]{0,1:T(4,128)S(1)}, s32[16,3]{0,1:T(4,128)}, u32[]{:S(2)}) copy-start(s32[16,3]{0,1:T(4,128)} %param.12) | copy-start | bytes 580
  226.8 25.6 %all-to-all-start.3 = ((bf16[16,16,2560]{2,1,0:T(8,128)(2,1)}), bf16[16,16,2560]{2,1,0:T(8,128)(2,1)S(1)}, u32[]{:S(2)}, u32[]{:S(2)}) async-start(bf16[16,16,2560]{2,1,0:T(8,128)(2,1)} %bitcast.25), calls=%async_computation.4 | async-start | bytes 2621440 | tf_op jit(solution)/shard_map/all_to_all | solution.py:175
  232.8 45.8 %copy-start.6 = (bf16[16,7168]{1,0:T(8,128)(2,1)S(1)}, bf16[16,7168]{1,0:T(8,128)(2,1)}, u32[]{:S(2)}) copy-start(bf16[16,7168]{1,0:T(8,128)(2,1)} %hidden_ref.1) | copy-start | bytes 688132
  262.4 15.8 %all-to-all-start.2 = ((bf16[8,8,4608]{2,1,0:T(8,128)(2,1)}), bf16[8,8,4608]{2,1,0:T(8,128)(2,1)S(1)}, u32[]{:S(2)}, u32[]{:S(2)}) async-start(bf16[8,8,4608]{2,1,0:T(8,128)(2,1)} %bitcast.58), calls=%async_computation.3 | async-start | bytes 1179648 | tf_op jit(solution)/shard_map/all_to_all | solution.py:244
  267.6 17.0 %copy-start.4 = (bf16[32,64,512]{2,1,0:T(8,128)(2,1)S(1)}, bf16[32,64,512]{2,1,0:T(8,128)(2,1)}, u32[]{:S(2)}) copy-start(bf16[32,64,512]{2,1,0:T(8,128)(2,1)} %copy-done.3) | copy-start | bytes 6291460
  280.0 15.2 %all-to-all-start.4 = ((bf16[16,2,7168]{2,1,0:T(2,128)(2,1)}), bf16[16,2,7168]{2,1,0:T(2,128)(2,1)S(1)}, u32[]{:S(2)}, u32[]{:S(2)}) async-start(bf16[16,2,7168]{2,1,0:T(2,128)(2,1)} %all_to_all.24), calls=%async_computation.5 | async-start | bytes 917504 | tf_op jit(solution)/shard_map/all_to_all | solution.py:271
  286.6 9.5 %copy-start.1 = (bf16[32,64,512]{2,1,0:T(8,128)(2,1)S(1)}, bf16[32,64,512]{2,1,0:T(8,128)(2,1)}, u32[]{:S(2)}) copy-start(bf16[32,64,512]{2,1,0:T(8,128)(2,1)} %param.16) | copy-start | bytes 6291460
Sparse Core Ops, SparseCore 0:
  11.6 119.3 all-gather.1
  171.5 90.8 reduce-scatter.1

commit v5 on v4

--- a/solution.py
+++ b/solution.py
@@ -222,14 +222,17 @@
     )
     kept_mask = (positions[None, :, :] < req_len[sources][:, None, None]) & occupied[:, None, None]
     outgoing_pages = jnp.where(kept_mask[..., None], page_rows, jnp.zeros_like(page_rows))
-    first_pages = lax.all_to_all(outgoing_pages[:, 0], "attn", split_axis=0, concat_axis=0, tiled=True)
     main = width - 2560
     swap = [(m, m ^ 1) for m in range(members)]
     weight_out = expert_out.reshape(expert_out.shape[1], width)
     side_out = weight_out[:, main:]
     side_out = jnp.concatenate([side_out, lax.ppermute(side_out, "ffn", swap)], axis=0)
+    first_out, second_out, side_out = lax.optimization_barrier(
+        (outgoing_pages[:, 0], outgoing_pages[:, 1], side_out)
+    )
+    first_pages = lax.all_to_all(first_out, "attn", split_axis=0, concat_axis=0, tiled=True)
     gathered, first_pages, second_out, side_out = lax.optimization_barrier(
-        (gathered, first_pages, outgoing_pages[:, 1], side_out)
+        (gathered, first_pages, second_out, side_out)
     )
     second_pages = lax.all_to_all(second_out, "attn", split_axis=0, concat_axis=0, tiled=True)
     member = lax.axis_index("ffn").astype(jnp.int32).reshape(1)

time: 304 us -> 297 us (0.977)
  blocking collectives: 0 us -> 42.3 us
  waiting for transfers between devices: 188 us -> 148 us
  starting transfers between devices: 31.3 us -> 23.9 us
    all_to_all x0 -> x1, blocking collectives: none -> 42.3 us  [body(): lax.all_to_all(first_out, 'attn', split_axis=0, concat_axis=0, tiled=True)]
    all_to_all x1 -> x0, waiting for transfers between devices: 31.8 us -> none  [body(): lax.all_to_all(outgoing_pages[:, 0], 'attn', split_axis=0, concat_axis=0,...]
    all_gather x1, waiting for transfers between devices: 66.2 us -> 57.7 us  [body(): gathered = lax.all_gather(payload, ('attn', 'ffn'), axis=0, tiled=True)]
    all_to_all x1 -> x0, starting transfers between devices: 7.12 us -> none  [body(): lax.all_to_all(outgoing_pages[:, 0], 'attn', split_axis=0, concat_axis=0,...]
  transfers between devices with their start and end apart: 15 -> 14, of which waited for: 14 -> 13; matrix products, arithmetic and copies ran while one was open for 11% -> 11% of each run, Pallas kernels for 11% -> 11%
where the time goes in v5:
time: 297 us
  waiting for transfers between devices  148 us (50%)
  blocking collectives  42.3 us (14%)
  Pallas kernels  34.4 us (12%)
  starting transfers between devices  23.9 us (8%)
  local copies, waits for them, and re-layouts  14.6 us (5%)
  between operations  14.4 us (5%)
  other arithmetic  11.5 us (4%)
  matrix products  8.04 us (3%)
    all_gather x1, waiting for transfers between devices, body(): gathered = lax.all_gather(payload, ('attn', 'ffn'), axis=0, tiled=True)  57.7 us
    all_to_all x1, blocking collectives, body(): lax.all_to_all(first_out, 'attn', split_axis=0, concat_axis=0, tiled=True)  42.3 us
    ppermute x6, waiting for transfers between devices, ring_sum(): arrived = lax.ppermute(total.astype(jnp.bfloat16), 'ffn', ring)  40.9 us
    pallas_call x1, Pallas kernels, run_experts(): pl.pallas_call(functools.partial(expert_kernel, hidden_dev, req_dev, cap,...  32.4 us
    all_to_all x1, waiting for transfers between devices, reduce_side(): lax.all_to_all(total.reshape(instances, req_dev, cols), 'attn', split_axi...  19.5 us
    all_to_all x1, waiting for transfers between devices, body(): lax.all_to_all(results, 'ffn', split_axis=0, concat_axis=0, tiled=True)  10.6 us
    reduce_scatter x1, waiting for transfers between devices, body(): summed = lax.psum_scatter(partial, 'attn', scatter_dimension=0, tiled=True)  9.45 us
    dot_general x8, matrix products, part(): jnp.dot(rows, weight_out[:, span], preferred_element_type=jnp.float32)  7.25 us
  transfers between devices with their start and end apart: 14, of which 13 were waited for; matrix products, arithmetic and copies ran while one was open for 11% of the time, Pallas kernels for 11%

profile of v5, /device:TPU:0, one launch (start us, length us, event | category | flops | bytes accessed | tf_op | source)
XLA Modules:
  0.0 296.9 jit_solution(2509692768033763923)
XLA Ops:
  7.3 2.0 shard_map.113
  9.3 2.7 slice.34
  14.1 2.8 gather_fusion.2
  17.2 2.6 broadcast_select_fusion
  19.8 1.6 slice_bitcast_fusion
  21.4 3.8 %pad_maximum_fusion.1 = bf16[640,2560]{1,0:T(8,128)(2,1)} fusion(bf16[320,2560]{1,0:T(8,128)(2,1)} %collective-permute-done, bf16[320,2560]{1,0:T(8,128)(2,1)} %slice.34), kind=kLoop, calls=%fused_computation.6 | loop fusion | flops 6553600 | bytes 6553600 | tf_op jit(solution)/shard_map/concatenate | solution.py:229
  25.2 42.3 %all_to_all.32 = bf16[32,64,512]{2,1,0:T(8,128)(2,1)} all-to-all(bf16[32,64,512]{2,1,0:T(8,128)(2,1)S(1)} %get-tuple-element.18), channel_id=1, replica_groups=mesh['attn'=16,'ffn'=8] {'attn'}, dimensions={0} | all-to-all | bytes 4194304 | tf_op jit(solution)/shard_map/all_to_all | solution.py:233
  67.6 57.7 %all-gather.2.cloned.1.call-done.lanes_ref.rows_ref = bf16[2048,7296]{1,0:T(8,128)(2,1)} async-done(((bf16[16,7296]{1,0:T(8,128)(2,1)}), bf16[2048,7296]{1,0:T(8,128)(2,1)}) %all-gather.2.cloned.1.call-update) | async-done | bytes 29884432 | tf_op jit(solution)/shard_map/all_gather | solution.py:204
  125.2 6.8 %all-to-all-start.1 = ((bf16[32,64,512]{2,1,0:T(8,128)(2,1)}), bf16[32,64,512]{2,1,0:T(8,128)(2,1)}, u32[]{:S(2)}, u32[]{:S(2)}) async-start(bf16[32,64,512]{2,1,0:T(8,128)(2,1)} %get-tuple-element.25), calls=%async_computation.1 | async-start | bytes 4194304 | tf_op jit(solution)/shard_map/all_to_all | solution.py:237
  132.1 32.4 %shard_map.114 = (bf16[1024,4608]{1,0:T(8,128)(2,1)}, bf16[2048,320]{1,0:T(8,128)(2,1)S(1)}) custom-call(s32[1]{0:T(128)} %bitcast.13.member_ref, bf16[2048,7296]{1,0:T(8,128)(2,1)} %all-gather.2.cloned.1.call-done.lanes_ref.rows_ref, bf16[2048,7296]{1,0:T(8,128)(2,1)} %all-gather.2.cloned.1.call-done.lanes_ref.rows_ref, bf16[640,7168]{1,0:T(8,128)(2,1)} %bitcast.54, ...), custom_call_target="tpu_custom_call" | custom-call | flops 16173236224 | bytes 52756480 | tf_op jit(solution)/shard_map/pallas_call | solution.py:121
  164.5 1.1 all-to-all-done.1
  165.6 1.1 dynamic-slice_bitcast_fusion
  166.7 2.5 collective-permute-done.1
  169.7 2.4 convolution_convert_fusion.2
  172.9 1.5 collective-permute-start.5
  174.4 9.6 %collective-permute-done.2 = bf16[256,1280]{1,0:T(8,128)(2,1)S(1)} collective-permute-done((bf16[256,1280]{1,0:T(8,128)(2,1)S(1)}, bf16[256,1280]{1,0:T(8,128)(2,1)S(1)}, u32[]{:S(2)}, u32[]{:S(2)}) %collective-permute-start.2) | collective-permute-done | bytes 655392 | tf_op jit(solution)/shard_map/ppermute | solution.py:170
  184.8 6.2 %collective-permute-done.5 = bf16[256,1280]{1,0:T(8,128)(2,1)S(1)} collective-permute-done((bf16[256,1280]{1,0:T(8,128)(2,1)S(1)}, bf16[256,1280]{1,0:T(8,128)(2,1)S(1)}, u32[]{:S(2)}, u32[]{:S(2)}) %collective-permute-start.5) | collective-permute-done | bytes 655392 | tf_op jit(solution)/shard_map/ppermute | solution.py:170
  191.8 6.2 %collective-permute-done.3 = bf16[256,1280]{1,0:T(8,128)(2,1)S(1)} collective-permute-done((bf16[256,1280]{1,0:T(8,128)(2,1)S(1)}, bf16[256,1280]{1,0:T(8,128)(2,1)S(1)}, u32[]{:S(2)}, u32[]{:S(2)}) %collective-permute-start.3) | collective-permute-done | bytes 655392 | tf_op jit(solution)/shard_map/ppermute | solution.py:170
  198.8 6.2 %collective-permute-done.6 = bf16[256,1280]{1,0:T(8,128)(2,1)S(1)} collective-permute-done((bf16[256,1280]{1,0:T(8,128)(2,1)S(1)}, bf16[256,1280]{1,0:T(8,128)(2,1)S(1)}, u32[]{:S(2)}, u32[]{:S(2)}) %collective-permute-start.6) | collective-permute-done | bytes 655392 | tf_op jit(solution)/shard_map/ppermute | solution.py:170
  205.8 6.2 %collective-permute-done.4 = bf16[256,1280]{1,0:T(8,128)(2,1)S(1)} collective-permute-done((bf16[256,1280]{1,0:T(8,128)(2,1)S(1)}, bf16[256,1280]{1,0:T(8,128)(2,1)S(1)}, u32[]{:S(2)}, u32[]{:S(2)}) %collective-permute-start.4) | collective-permute-done | bytes 655392 | tf_op jit(solution)/shard_map/ppermute | solution.py:170
  212.8 6.3 %collective-permute-done.7 = bf16[256,1280]{1,0:T(8,128)(2,1)S(1)} collective-permute-done((bf16[256,1280]{1,0:T(8,128)(2,1)S(1)}, bf16[256,1280]{1,0:T(8,128)(2,1)S(1)}, u32[]{:S(2)}, u32[]{:S(2)}) %collective-permute-start.7) | collective-permute-done | bytes 655392 | tf_op jit(solution)/shard_map/ppermute | solution.py:170
  219.8 1.1 pad_maximum_fusion.2
  221.0 6.0 %all-to-all-start.3 = ((bf16[16,16,2560]{2,1,0:T(8,128)(2,1)}), bf16[16,16,2560]{2,1,0:T(8,128)(2,1)S(1)}, u32[]{:S(2)}, u32[]{:S(2)}) async-start(bf16[16,16,2560]{2,1,0:T(8,128)(2,1)} %bitcast.25), calls=%async_computation.4 | async-start | bytes 2621440 | tf_op jit(solution)/shard_map/all_to_all | solution.py:175
  227.7 19.5 %all-to-all-done.3 = bf16[16,16,2560]{2,1,0:T(8,128)(2,1)S(1)} async-done(((bf16[16,16,2560]{2,1,0:T(8,128)(2,1)}), bf16[16,16,2560]{2,1,0:T(8,128)(2,1)S(1)}, u32[]{:S(2)}, u32[]{:S(2)}) %all-to-all-start.3) | async-done | bytes 1310752 | tf_op jit(solution)/shard_map/all_to_all | solution.py:175
  247.2 9.4 %reduce-scatter.2.cloned.1.call-done = bf16[64,4608]{1,0:T(8,128)(2,1)} async-done(((bf16[1024,4608]{1,0:T(8,128)(2,1)}), bf16[64,4608]{1,0:T(8,128)(2,1)}) %reduce-scatter.2.cloned.1.call-update) | async-done | bytes 589840 | tf_op jit(solution)/shard_map/reduce_scatter | solution.py:245
  256.7 4.2 %all-to-all-start.2 = ((bf16[8,8,4608]{2,1,0:T(8,128)(2,1)}), bf16[8,8,4608]{2,1,0:T(8,128)(2,1)S(1)}, u32[]{:S(2)}, u32[]{:S(2)}) async-start(bf16[8,8,4608]{2,1,0:T(8,128)(2,1)} %bitcast.58), calls=%async_computation.3 | async-start | bytes 1179648 | tf_op jit(solution)/shard_map/all_to_all | solution.py:247
  261.3 10.6 %all-to-all-done.2 = bf16[8,8,4608]{2,1,0:T(8,128)(2,1)S(1)} async-done(((bf16[8,8,4608]{2,1,0:T(8,128)(2,1)}), bf16[8,8,4608]{2,1,0:T(8,128)(2,1)S(1)}, u32[]{:S(2)}, u32[]{:S(2)}) %all-to-all-start.2) | async-done | bytes 589856 | tf_op jit(solution)/shard_map/all_to_all | solution.py:247
  272.7 0.9 all_to_all.24
  273.7 4.9 %all-to-all-start.4 = ((bf16[16,2,7168]{2,1,0:T(2,128)(2,1)}), bf16[16,2,7168]{2,1,0:T(2,128)(2,1)S(1)}, u32[]{:S(2)}, u32[]{:S(2)}) async-start(bf16[16,2,7168]{2,1,0:T(2,128)(2,1)} %all_to_all.24), calls=%async_computation.5 | async-start | bytes 917504 | tf_op jit(solution)/shard_map/all_to_all | solution.py:274
  278.6 2.0 pad_maximum_fusion
  280.6 2.5 copy.31
  283.1 6.1 %all-to-all-done.4 = bf16[16,2,7168]{2,1,0:T(2,128)(2,1)S(1)} async-done(((bf16[16,2,7168]{2,1,0:T(2,128)(2,1)}), bf16[16,2,7168]{2,1,0:T(2,128)(2,1)S(1)}, u32[]{:S(2)}, u32[]{:S(2)}) %all-to-all-start.4) | async-done | bytes 458784 | tf_op jit(solution)/shard_map/all_to_all | solution.py:274
  (72 shorter events, 11.1 us)
Async XLA Ops:
  7.2 6.9 %copy-start = (bf16[32,64,512]{2,1,0:T(8,128)(2,1)S(1)}, bf16[32,64,512]{2,1,0:T(8,128)(2,1)}, u32[]{:S(2)}) copy-start(bf16[32,64,512]{2,1,0:T(8,128)(2,1)} %param.16) | copy-start | bytes 6291460
  7.2 4.8 %copy-start.9 = (s32[16,2]{0,1:T(2,128)S(1)}, s32[16,2]{0,1:T(2,128)}, u32[]{:S(2)}) copy-start(s32[16,2]{0,1:T(2,128)} %param.17) | copy-start | bytes 388
  7.2 4.9 %copy-start.8 = (s32[16,1]{0,1:T(1,128)S(1)}, s32[16,1]{0,1:T(1,128)}, u32[]{:S(2)}) copy-start(s32[16,1]{0,1:T(1,128)} %param.19) | copy-start | bytes 196
  7.2 118.0 %all-gather.2.cloned.1.call-start = ((), (), s32[]{:S(2)}) async-start(), calls=%async_computation.6 | async-start | bytes 30117888 | tf_op jit(solution)/shard_map/all_gather | solution.py:204
  7.2 5.9 %copy-start.2 = (s32[16]{0:T(128)S(1)}, s32[16]{0:T(128)}, u32[]{:S(2)}) copy-start(s32[16]{0:T(128)} %param.18) | copy-start | bytes 196
  12.0 9.4 %collective-permute-start = (bf16[320,2560]{1,0:T(8,128)(2,1)}, bf16[320,2560]{1,0:T(8,128)(2,1)}, u32[]{:S(2)}, u32[]{:S(2)}) collective-permute-start(bf16[320,2560]{1,0:T(8,128)(2,1)} %slice.34), channel_id=1, source_target_pairs={{0,1},{1,0},{2,3},{3,2},{4,5},{5,4},{6,7},{7,6},{8,9},{9,8},{10,11... | collective-permute-start | bytes 4915208 | tf_op jit(solution)/shard_map/ppermute | solution.py:229
  125.2 40.4 %all-to-all-start.1 = ((bf16[32,64,512]{2,1,0:T(8,128)(2,1)}), bf16[32,64,512]{2,1,0:T(8,128)(2,1)}, u32[]{:S(2)}, u32[]{:S(2)}) async-start(bf16[32,64,512]{2,1,0:T(8,128)(2,1)} %get-tuple-element.25), calls=%async_computation.1 | async-start | bytes 4194304 | tf_op jit(solution)/shard_map/all_to_all | solution.py:237
  132.1 124.6 %reduce-scatter.2.cloned.1.call-start = ((), (), s32[]{:S(2)}) async-start(), calls=%async_computation.7 | async-start | bytes 10027008 | tf_op jit(solution)/shard_map/reduce_scatter | solution.py:245
  166.7 2.5 collective-permute-start.1
  169.2 3.0 %copy-start.4 = (bf16[640,2560]{1,0:T(8,128)(2,1)S(1)}, bf16[640,2560]{1,0:T(8,128)(2,1)}, u32[]{:S(2)}) copy-start(bf16[640,2560]{1,0:T(8,128)(2,1)} %pad_maximum_fusion.1) | copy-start | bytes 9830404
  172.1 11.9 %collective-permute-start.2 = (bf16[256,1280]{1,0:T(8,128)(2,1)S(1)}, bf16[256,1280]{1,0:T(8,128)(2,1)S(1)}, u32[]{:S(2)}, u32[]{:S(2)}) collective-permute-start(bf16[256,1280]{1,0:T(8,128)(2,1)S(1)} %convolution_convert_fusion.2), channel_id=1, source_target_pairs={{0,2},{1,7},{2,4},{3,1},{4,6},{5,3},{6,0},{7,5},{8,10},{9,15},{10,... | collective-permute-start | bytes 1966088 | tf_op jit(solution)/shard_map/ppermute | solution.py:170
  172.9 18.1 %collective-permute-start.5 = (bf16[256,1280]{1,0:T(8,128)(2,1)S(1)}, bf16[256,1280]{1,0:T(8,128)(2,1)S(1)}, u32[]{:S(2)}, u32[]{:S(2)}) collective-permute-start(bf16[256,1280]{1,0:T(8,128)(2,1)S(1)} %convolution_convert_fusion.1), channel_id=1, source_target_pairs={{0,2},{1,7},{2,4},{3,1},{4,6},{5,3},{6,0},{7,5},{8,10},{9,15},{10,... | collective-permute-start | bytes 1966088 | tf_op jit(solution)/shard_map/ppermute | solution.py:170
  184.7 13.3 %collective-permute-start.3 = (bf16[256,1280]{1,0:T(8,128)(2,1)S(1)}, bf16[256,1280]{1,0:T(8,128)(2,1)S(1)}, u32[]{:S(2)}, u32[]{:S(2)}) collective-permute-start(bf16[256,1280]{1,0:T(8,128)(2,1)S(1)} %add_convert_fusion.5), channel_id=1, source_target_pairs={{0,2},{1,7},{2,4},{3,1},{4,6},{5,3},{6,0},{7,5},{8,10},{9,15},{10,... | collective-permute-start | bytes 1966088 | tf_op jit(solution)/shard_map/ppermute | solution.py:170
  191.7 13.3 %collective-permute-start.6 = (bf16[256,1280]{1,0:T(8,128)(2,1)S(1)}, bf16[256,1280]{1,0:T(8,128)(2,1)S(1)}, u32[]{:S(2)}, u32[]{:S(2)}) collective-permute-start(bf16[256,1280]{1,0:T(8,128)(2,1)S(1)} %add_convert_fusion.2), channel_id=1, source_target_pairs={{0,2},{1,7},{2,4},{3,1},{4,6},{5,3},{6,0},{7,5},{8,10},{9,15},{10,... | collective-permute-start | bytes 1966088 | tf_op jit(solution)/shard_map/ppermute | solution.py:170
  198.7 13.3 %collective-permute-start.4 = (bf16[256,1280]{1,0:T(8,128)(2,1)S(1)}, bf16[256,1280]{1,0:T(8,128)(2,1)S(1)}, u32[]{:S(2)}, u32[]{:S(2)}) collective-permute-start(bf16[256,1280]{1,0:T(8,128)(2,1)S(1)} %add_convert_fusion.4), channel_id=1, source_target_pairs={{0,2},{1,7},{2,4},{3,1},{4,6},{5,3},{6,0},{7,5},{8,10},{9,15},{10,... | collective-permute-start | bytes 1966088 | tf_op jit(solution)/shard_map/ppermute | solution.py:170
  205.7 13.3 %collective-permute-start.7 = (bf16[256,1280]{1,0:T(8,128)(2,1)S(1)}, bf16[256,1280]{1,0:T(8,128)(2,1)S(1)}, u32[]{:S(2)}, u32[]{:S(2)}) collective-permute-start(bf16[256,1280]{1,0:T(8,128)(2,1)S(1)} %add_convert_fusion.1), channel_id=1, source_target_pairs={{0,2},{1,7},{2,4},{3,1},{4,6},{5,3},{6,0},{7,5},{8,10},{9,15},{10,... | collective-permute-start | bytes 1966088 | tf_op jit(solution)/shard_map/ppermute | solution.py:170
  219.8 7.2 %copy-start.6 = (s32[16,3]{0,1:T(4,128)S(1)}, s32[16,3]{0,1:T(4,128)}, u32[]{:S(2)}) copy-start(s32[16,3]{0,1:T(4,128)} %param.12) | copy-start | bytes 580
  219.8 7.3 %copy-start.7 = (f32[16,3]{0,1:T(4,128)S(1)}, f32[16,3]{0,1:T(4,128)}, u32[]{:S(2)}) copy-start(f32[16,3]{0,1:T(4,128)} %param.13) | copy-start | bytes 580
  221.0 26.3 %all-to-all-start.3 = ((bf16[16,16,2560]{2,1,0:T(8,128)(2,1)}), bf16[16,16,2560]{2,1,0:T(8,128)(2,1)S(1)}, u32[]{:S(2)}, u32[]{:S(2)}) async-start(bf16[16,16,2560]{2,1,0:T(8,128)(2,1)} %bitcast.25), calls=%async_computation.4 | async-start | bytes 2621440 | tf_op jit(solution)/shard_map/all_to_all | solution.py:175
  227.0 45.3 %copy-start.5 = (bf16[16,7168]{1,0:T(8,128)(2,1)S(1)}, bf16[16,7168]{1,0:T(8,128)(2,1)}, u32[]{:S(2)}) copy-start(bf16[16,7168]{1,0:T(8,128)(2,1)} %hidden_ref.1) | copy-start | bytes 688132
  256.7 15.2 %all-to-all-start.2 = ((bf16[8,8,4608]{2,1,0:T(8,128)(2,1)}), bf16[8,8,4608]{2,1,0:T(8,128)(2,1)S(1)}, u32[]{:S(2)}, u32[]{:S(2)}) async-start(bf16[8,8,4608]{2,1,0:T(8,128)(2,1)} %bitcast.58), calls=%async_computation.3 | async-start | bytes 1179648 | tf_op jit(solution)/shard_map/all_to_all | solution.py:247
  261.3 17.3 %copy-start.3 = (bf16[32,64,512]{2,1,0:T(8,128)(2,1)S(1)}, bf16[32,64,512]{2,1,0:T(8,128)(2,1)}, u32[]{:S(2)}) copy-start(bf16[32,64,512]{2,1,0:T(8,128)(2,1)} %all_to_all.32) | copy-start | bytes 6291460
  273.7 15.5 %all-to-all-start.4 = ((bf16[16,2,7168]{2,1,0:T(2,128)(2,1)}), bf16[16,2,7168]{2,1,0:T(2,128)(2,1)S(1)}, u32[]{:S(2)}, u32[]{:S(2)}) async-start(bf16[16,2,7168]{2,1,0:T(2,128)(2,1)} %all_to_all.24), calls=%async_computation.5 | async-start | bytes 917504 | tf_op jit(solution)/shard_map/all_to_all | solution.py:274
  280.6 9.5 %copy-start.1 = (bf16[32,64,512]{2,1,0:T(8,128)(2,1)S(1)}, bf16[32,64,512]{2,1,0:T(8,128)(2,1)}, u32[]{:S(2)}) copy-start(bf16[32,64,512]{2,1,0:T(8,128)(2,1)} %param.16) | copy-start | bytes 6291460
Sparse Core Ops, SparseCore 0:
  11.6 113.5 all-gather.1
  165.7 90.9 reduce-scatter.1

commit v6 on v4

--- a/solution.py
+++ b/solution.py
@@ -8,7 +8,6 @@
 from jax.sharding import PartitionSpec as P
 
 PAGE = 64
-PAGES_REQ = 2
 ID_LANES = 128
 MIB = 1 << 20
 
@@ -84,12 +83,17 @@
     def _():
         gate = acc_ref[:, :hidden_dev]
         act_ref[...] = (gate / (1.0 + jnp.exp(-gate)) * acc_ref[:, hidden_dev : 2 * hidden_dev]).astype(jnp.bfloat16)
+        source = lax.broadcasted_iota(jnp.int32, (ID_LANES, ID_LANES), 0)
+        target = lax.broadcasted_iota(jnp.int32, (ID_LANES, ID_LANES), 1)
+        moved = (target == source + topk) | (target == source + 2 * topk)
+        shift = jnp.where(moved & (source < topk), 1.0, 0.0).astype(jnp.bfloat16)
+        ones = jnp.ones((ID_LANES, hidden_dev), jnp.bfloat16)
+        lane = lax.broadcasted_iota(jnp.int32, (rows, ID_LANES), 1)
         for group in range(groups):
             lanes = lanes_ref[group * rows : (group + 1) * rows, :].astype(jnp.float32)
-            score = jnp.zeros((rows, 1), jnp.float32)
-            for k in range(topk):
-                high, low = (lanes[:, n * topk + k : n * topk + k + 1] for n in (1, 2))
-                score = jnp.where(lanes[:, k : k + 1] == member, high + low, score)
+            named = jnp.where((lanes == member) & (lane < topk), 1.0, 0.0).astype(jnp.bfloat16)
+            parts = (jnp.dot(named, shift, preferred_element_type=jnp.float32) * lanes).astype(jnp.bfloat16)
+            score = jnp.dot(parts, ones, preferred_element_type=jnp.float32)
             back = jnp.dot(
                 chosen_ref[group], act_ref[group * slots : (group + 1) * slots, :], preferred_element_type=jnp.float32
             )
@@ -215,21 +219,23 @@
         routing.astype(jnp.int32) * jnp.arange(req_dev, dtype=jnp.int32)[None, :], axis=1
     )
     tables = block_table[sources]
-    page_rows = kv_pages[tables]
-    positions = (
-        jnp.arange(PAGES_REQ, dtype=jnp.int32)[:, None] * PAGE
-        + jnp.arange(PAGE, dtype=jnp.int32)[None, :]
-    )
-    kept_mask = (positions[None, :, :] < req_len[sources][:, None, None]) & occupied[:, None, None]
-    outgoing_pages = jnp.where(kept_mask[..., None], page_rows, jnp.zeros_like(page_rows))
-    first_pages = lax.all_to_all(outgoing_pages[:, 0], "attn", split_axis=0, concat_axis=0, tiled=True)
+    def pages_out(pages, which):
+        positions = which * PAGE + jnp.arange(PAGE, dtype=jnp.int32)
+        kept_mask = (positions[None, :] < req_len[sources][:, None]) & occupied[:, None]
+        page_rows = pages[tables[:, which]]
+        return jnp.where(kept_mask[..., None], page_rows, jnp.zeros_like(page_rows))
+
+    first_pages = lax.all_to_all(pages_out(kv_pages, 0), "attn", split_axis=0, concat_axis=0, tiled=True)
+    first_pages, kv_pages, expert_out = lax.optimization_barrier((first_pages, kv_pages, expert_out))
+    second_out = pages_out(kv_pages, 1)
+
     main = width - 2560
     swap = [(m, m ^ 1) for m in range(members)]
     weight_out = expert_out.reshape(expert_out.shape[1], width)
     side_out = weight_out[:, main:]
     side_out = jnp.concatenate([side_out, lax.ppermute(side_out, "ffn", swap)], axis=0)
     gathered, first_pages, second_out, side_out = lax.optimization_barrier(
-        (gathered, first_pages, outgoing_pages[:, 1], side_out)
+        (gathered, first_pages, second_out, side_out)
     )
     second_pages = lax.all_to_all(second_out, "attn", split_axis=0, concat_axis=0, tiled=True)
     member = lax.axis_index("ffn").astype(jnp.int32).reshape(1)

time: 304 us -> 297 us (0.977)
  waiting for transfers between devices: 188 us -> 149 us
  blocking collectives: 0 us -> 37.5 us
  starting transfers between devices: 31.3 us -> 22.6 us
  other arithmetic: 11.6 us -> 18.5 us
    all_to_all x0 -> x1, blocking collectives: none -> 37.5 us  [body(): lax.all_to_all(pages_out(kv_pages, 0), 'attn', split_axis=0, concat_axis=...]
    all_to_all x1 -> x0, waiting for transfers between devices: 31.8 us -> none  [body(): lax.all_to_all(outgoing_pages[:, 0], 'attn', split_axis=0, concat_axis=0,...]
    all_gather x1, waiting for transfers between devices: 66.2 us -> 58.2 us  [body(): gathered = lax.all_gather(payload, ('attn', 'ffn'), axis=0, tiled=True)]
    all_to_all x1 -> x0, starting transfers between devices: 7.12 us -> none  [body(): lax.all_to_all(outgoing_pages[:, 0], 'attn', split_axis=0, concat_axis=0,...]
  transfers between devices with their start and end apart: 15 -> 14, of which waited for: 14 -> 13; matrix products, arithmetic and copies ran while one was open for 11% -> 12% of each run, Pallas kernels for 11% -> 11%
where the time goes in v6:
time: 297 us; the launch traced here: 296 us
  waiting for transfers between devices  149 us (50%)
  blocking collectives  37.5 us (13%)
  Pallas kernels  33.3 us (11%)
  starting transfers between devices  22.6 us (8%)
  other arithmetic  18.5 us (6%)
  between operations  14.3 us (5%)
  local copies, waits for them, and re-layouts  12.8 us (4%)
  matrix products  8.05 us (3%)
    all_gather x1, waiting for transfers between devices, body(): gathered = lax.all_gather(payload, ('attn', 'ffn'), axis=0, tiled=True)  58.2 us
    ppermute x6, waiting for transfers between devices, ring_sum(): arrived = lax.ppermute(total.astype(jnp.bfloat16), 'ffn', ring)  40.8 us
    all_to_all x1, blocking collectives, body(): lax.all_to_all(pages_out(kv_pages, 0), 'attn', split_axis=0, concat_axis=...  37.5 us
    pallas_call x1, Pallas kernels, run_experts(): pl.pallas_call(functools.partial(expert_kernel, hidden_dev, req_dev, cap,...  31.3 us
    all_to_all x1, waiting for transfers between devices, reduce_side(): lax.all_to_all(total.reshape(instances, req_dev, cols), 'attn', split_axi...  19.8 us
    all_to_all x1, waiting for transfers between devices, body(): lax.all_to_all(results, 'ffn', split_axis=0, concat_axis=0, tiled=True)  10.6 us
    reduce_scatter x1, waiting for transfers between devices, body(): summed = lax.psum_scatter(partial, 'attn', scatter_dimension=0, tiled=True)  9.33 us
    dot_general x8, matrix products, part(): jnp.dot(rows, weight_out[:, span], preferred_element_type=jnp.float32)  7.25 us
  transfers between devices with their start and end apart: 14, of which 13 were waited for; matrix products, arithmetic and copies ran while one was open for 12% of the time, Pallas kernels for 11%

profile of v6, /device:TPU:0, one launch (start us, length us, event | category | flops | bytes accessed | tf_op | source)
XLA Modules:
  0.0 296.4 jit_solution(5936413147713088621)
XLA Ops:
  7.2 2.0 shard_map.113
  13.2 1.4 gather_fusion
  14.7 2.0 gather_fusion.2
  16.9 1.8 broadcast_select_fusion.1
  18.7 37.5 %all_to_all.32 = bf16[32,64,512]{2,1,0:T(8,128)(2,1)} all-to-all(bf16[32,64,512]{2,1,0:T(8,128)(2,1)S(1)} %broadcast_select_fusion.1), channel_id=1, replica_groups=mesh['attn'=16,'ffn'=8] {'attn'}, dimensions={0} | all-to-all | bytes 4194304 | tf_op jit(solution)/shard_map/all_to_all | solution.py:228
  56.2 2.7 slice.36
  59.0 2.0 gather_fusion.3
  61.0 2.8 broadcast_select_fusion
  63.7 3.9 %pad_maximum_fusion.1 = bf16[640,2560]{1,0:T(8,128)(2,1)} fusion(bf16[320,2560]{1,0:T(8,128)(2,1)} %collective-permute-done, bf16[320,2560]{1,0:T(8,128)(2,1)} %slice.36), kind=kLoop, calls=%fused_computation.6 | loop fusion | flops 6553600 | bytes 6553600 | tf_op jit(solution)/shard_map/concatenate | solution.py:236
  67.7 58.2 %all-gather.2.cloned.1.call-done.lanes_ref.rows_ref = bf16[2048,7296]{1,0:T(8,128)(2,1)} async-done(((bf16[16,7296]{1,0:T(8,128)(2,1)}), bf16[2048,7296]{1,0:T(8,128)(2,1)}) %all-gather.2.cloned.1.call-update) | async-done | bytes 29884432 | tf_op jit(solution)/shard_map/all_gather | solution.py:208
  125.8 6.8 %all-to-all-start.1 = ((bf16[32,64,512]{2,1,0:T(8,128)(2,1)}), bf16[32,64,512]{2,1,0:T(8,128)(2,1)}, u32[]{:S(2)}, u32[]{:S(2)}) async-start(bf16[32,64,512]{2,1,0:T(8,128)(2,1)} %broadcast_select_fusion), calls=%async_computation.1 | async-start | bytes 4194304 | tf_op jit(solution)/shard_map/all_to_all | solution.py:240
  132.7 31.3 %shard_map.114 = (bf16[1024,4608]{1,0:T(8,128)(2,1)}, bf16[2048,320]{1,0:T(8,128)(2,1)S(1)}) custom-call(s32[1]{0:T(128)} %bitcast.9.member_ref, bf16[2048,7296]{1,0:T(8,128)(2,1)} %all-gather.2.cloned.1.call-done.lanes_ref.rows_ref, bf16[2048,7296]{1,0:T(8,128)(2,1)} %all-gather.2.cloned.1.call-done.lanes_ref.rows_ref, bf16[640,7168]{1,0:T(8,128)(2,1)} %bitcast.41, ...), custom_call_target="tpu_custom_call" | custom-call | flops 16173236224 | bytes 52756480 | tf_op jit(solution)/shard_map/pallas_call | solution.py:125
  164.0 2.2 all-to-all-done.1
  166.2 1.1 dynamic-slice_bitcast_fusion
  167.3 2.5 collective-permute-done.1
  170.3 2.4 convolution_convert_fusion.2
  173.5 1.3 collective-permute-start.5
  174.8 9.8 %collective-permute-done.2 = bf16[256,1280]{1,0:T(8,128)(2,1)S(1)} collective-permute-done((bf16[256,1280]{1,0:T(8,128)(2,1)S(1)}, bf16[256,1280]{1,0:T(8,128)(2,1)S(1)}, u32[]{:S(2)}, u32[]{:S(2)}) %collective-permute-start.2) | collective-permute-done | bytes 655392 | tf_op jit(solution)/shard_map/ppermute | solution.py:174
  185.5 6.0 %collective-permute-done.5 = bf16[256,1280]{1,0:T(8,128)(2,1)S(1)} collective-permute-done((bf16[256,1280]{1,0:T(8,128)(2,1)S(1)}, bf16[256,1280]{1,0:T(8,128)(2,1)S(1)}, u32[]{:S(2)}, u32[]{:S(2)}) %collective-permute-start.5) | collective-permute-done | bytes 655392 | tf_op jit(solution)/shard_map/ppermute | solution.py:174
  192.4 6.2 %collective-permute-done.3 = bf16[256,1280]{1,0:T(8,128)(2,1)S(1)} collective-permute-done((bf16[256,1280]{1,0:T(8,128)(2,1)S(1)}, bf16[256,1280]{1,0:T(8,128)(2,1)S(1)}, u32[]{:S(2)}, u32[]{:S(2)}) %collective-permute-start.3) | collective-permute-done | bytes 655392 | tf_op jit(solution)/shard_map/ppermute | solution.py:174
  199.4 6.2 %collective-permute-done.6 = bf16[256,1280]{1,0:T(8,128)(2,1)S(1)} collective-permute-done((bf16[256,1280]{1,0:T(8,128)(2,1)S(1)}, bf16[256,1280]{1,0:T(8,128)(2,1)S(1)}, u32[]{:S(2)}, u32[]{:S(2)}) %collective-permute-start.6) | collective-permute-done | bytes 655392 | tf_op jit(solution)/shard_map/ppermute | solution.py:174
  206.4 6.2 %collective-permute-done.4 = bf16[256,1280]{1,0:T(8,128)(2,1)S(1)} collective-permute-done((bf16[256,1280]{1,0:T(8,128)(2,1)S(1)}, bf16[256,1280]{1,0:T(8,128)(2,1)S(1)}, u32[]{:S(2)}, u32[]{:S(2)}) %collective-permute-start.4) | collective-permute-done | bytes 655392 | tf_op jit(solution)/shard_map/ppermute | solution.py:174
  213.4 6.3 %collective-permute-done.7 = bf16[256,1280]{1,0:T(8,128)(2,1)S(1)} collective-permute-done((bf16[256,1280]{1,0:T(8,128)(2,1)S(1)}, bf16[256,1280]{1,0:T(8,128)(2,1)S(1)}, u32[]{:S(2)}, u32[]{:S(2)}) %collective-permute-start.7) | collective-permute-done | bytes 655392 | tf_op jit(solution)/shard_map/ppermute | solution.py:174
  220.4 1.1 pad_maximum_fusion.2
  221.6 5.0 %all-to-all-start.3 = ((bf16[16,16,2560]{2,1,0:T(8,128)(2,1)}), bf16[16,16,2560]{2,1,0:T(8,128)(2,1)S(1)}, u32[]{:S(2)}, u32[]{:S(2)}) async-start(bf16[16,16,2560]{2,1,0:T(8,128)(2,1)} %bitcast.21), calls=%async_computation.4 | async-start | bytes 2621440 | tf_op jit(solution)/shard_map/all_to_all | solution.py:179
  227.3 19.8 %all-to-all-done.3 = bf16[16,16,2560]{2,1,0:T(8,128)(2,1)S(1)} async-done(((bf16[16,16,2560]{2,1,0:T(8,128)(2,1)}), bf16[16,16,2560]{2,1,0:T(8,128)(2,1)S(1)}, u32[]{:S(2)}, u32[]{:S(2)}) %all-to-all-start.3) | async-done | bytes 1310752 | tf_op jit(solution)/shard_map/all_to_all | solution.py:179
  247.1 9.3 %reduce-scatter.2.cloned.1.call-done = bf16[64,4608]{1,0:T(8,128)(2,1)} async-done(((bf16[1024,4608]{1,0:T(8,128)(2,1)}), bf16[64,4608]{1,0:T(8,128)(2,1)}) %reduce-scatter.2.cloned.1.call-update) | async-done | bytes 589840 | tf_op jit(solution)/shard_map/reduce_scatter | solution.py:248
  256.4 3.9 %all-to-all-start.2 = ((bf16[8,8,4608]{2,1,0:T(8,128)(2,1)}), bf16[8,8,4608]{2,1,0:T(8,128)(2,1)S(1)}, u32[]{:S(2)}, u32[]{:S(2)}) async-start(bf16[8,8,4608]{2,1,0:T(8,128)(2,1)} %bitcast.45), calls=%async_computation.3 | async-start | bytes 1179648 | tf_op jit(solution)/shard_map/all_to_all | solution.py:250
  260.7 10.6 %all-to-all-done.2 = bf16[8,8,4608]{2,1,0:T(8,128)(2,1)S(1)} async-done(((bf16[8,8,4608]{2,1,0:T(8,128)(2,1)}), bf16[8,8,4608]{2,1,0:T(8,128)(2,1)S(1)}, u32[]{:S(2)}, u32[]{:S(2)}) %all-to-all-start.2) | async-done | bytes 589856 | tf_op jit(solution)/shard_map/all_to_all | solution.py:250
  273.1 4.9 %all-to-all-start.4 = ((bf16[16,2,7168]{2,1,0:T(2,128)(2,1)}), bf16[16,2,7168]{2,1,0:T(2,128)(2,1)S(1)}, u32[]{:S(2)}, u32[]{:S(2)}) async-start(bf16[16,2,7168]{2,1,0:T(2,128)(2,1)} %all_to_all.24), calls=%async_computation.5 | async-start | bytes 917504 | tf_op jit(solution)/shard_map/all_to_all | solution.py:277
  278.0 4.8 %pad_maximum_fusion = bf16[32,2,64,512]{3,2,1,0:T(8,128)(2,1)} fusion(bf16[32,1,64,512]{3,2,1,0:T(8,128)(2,1)} %bitcast.11, bf16[32,1,64,512]{3,2,1,0:T(8,128)(2,1)} %bitcast.44), kind=kLoop, calls=%fused_computation.5 | loop fusion | flops 2097152 | bytes 8388608 | tf_op jit(solution)/shard_map/stack | solution.py:247
  282.8 5.8 %all-to-all-done.4 = bf16[16,2,7168]{2,1,0:T(2,128)(2,1)S(1)} async-done(((bf16[16,2,7168]{2,1,0:T(2,128)(2,1)}), bf16[16,2,7168]{2,1,0:T(2,128)(2,1)S(1)}, u32[]{:S(2)}, u32[]{:S(2)}) %all-to-all-start.4) | async-done | bytes 458784 | tf_op jit(solution)/shard_map/all_to_all | solution.py:277
  (61 shorter events, 14.1 us)
Async XLA Ops:
  7.2 7.5 %copy-start = (bf16[32,64,512]{2,1,0:T(8,128)(2,1)S(1)}, bf16[32,64,512]{2,1,0:T(8,128)(2,1)}, u32[]{:S(2)}) copy-start(bf16[32,64,512]{2,1,0:T(8,128)(2,1)} %param.16) | copy-start | bytes 6291460
  7.2 118.7 %all-gather.2.cloned.1.call-start = ((), (), s32[]{:S(2)}) async-start(), calls=%async_computation.6 | async-start | bytes 30117888 | tf_op jit(solution)/shard_map/all_gather | solution.py:208
  59.0 4.8 %collective-permute-start = (bf16[320,2560]{1,0:T(8,128)(2,1)}, bf16[320,2560]{1,0:T(8,128)(2,1)}, u32[]{:S(2)}, u32[]{:S(2)}) collective-permute-start(bf16[320,2560]{1,0:T(8,128)(2,1)} %slice.36), channel_id=1, source_target_pairs={{0,1},{1,0},{2,3},{3,2},{4,5},{5,4},{6,7},{7,6},{8,9},{9,8},{10,11... | collective-permute-start | bytes 4915208 | tf_op jit(solution)/shard_map/ppermute | solution.py:236
  125.8 40.4 %all-to-all-start.1 = ((bf16[32,64,512]{2,1,0:T(8,128)(2,1)}), bf16[32,64,512]{2,1,0:T(8,128)(2,1)}, u32[]{:S(2)}, u32[]{:S(2)}) async-start(bf16[32,64,512]{2,1,0:T(8,128)(2,1)} %broadcast_select_fusion), calls=%async_computation.1 | async-start | bytes 4194304 | tf_op jit(solution)/shard_map/all_to_all | solution.py:240
  132.7 123.7 %reduce-scatter.2.cloned.1.call-start = ((), (), s32[]{:S(2)}) async-start(), calls=%async_computation.7 | async-start | bytes 10027008 | tf_op jit(solution)/shard_map/reduce_scatter | solution.py:248
  167.3 2.5 collective-permute-start.1
  169.8 3.0 %copy-start.2 = (bf16[640,2560]{1,0:T(8,128)(2,1)S(1)}, bf16[640,2560]{1,0:T(8,128)(2,1)}, u32[]{:S(2)}) copy-start(bf16[640,2560]{1,0:T(8,128)(2,1)} %pad_maximum_fusion.1) | copy-start | bytes 9830404
  172.7 11.9 %collective-permute-start.2 = (bf16[256,1280]{1,0:T(8,128)(2,1)S(1)}, bf16[256,1280]{1,0:T(8,128)(2,1)S(1)}, u32[]{:S(2)}, u32[]{:S(2)}) collective-permute-start(bf16[256,1280]{1,0:T(8,128)(2,1)S(1)} %convolution_convert_fusion.2), channel_id=1, source_target_pairs={{0,2},{1,7},{2,4},{3,1},{4,6},{5,3},{6,0},{7,5},{8,10},{9,15},{10,... | collective-permute-start | bytes 1966088 | tf_op jit(solution)/shard_map/ppermute | solution.py:174
  173.5 18.1 %collective-permute-start.5 = (bf16[256,1280]{1,0:T(8,128)(2,1)S(1)}, bf16[256,1280]{1,0:T(8,128)(2,1)S(1)}, u32[]{:S(2)}, u32[]{:S(2)}) collective-permute-start(bf16[256,1280]{1,0:T(8,128)(2,1)S(1)} %convolution_convert_fusion.1), channel_id=1, source_target_pairs={{0,2},{1,7},{2,4},{3,1},{4,6},{5,3},{6,0},{7,5},{8,10},{9,15},{10,... | collective-permute-start | bytes 1966088 | tf_op jit(solution)/shard_map/ppermute | solution.py:174
  185.3 13.3 %collective-permute-start.3 = (bf16[256,1280]{1,0:T(8,128)(2,1)S(1)}, bf16[256,1280]{1,0:T(8,128)(2,1)S(1)}, u32[]{:S(2)}, u32[]{:S(2)}) collective-permute-start(bf16[256,1280]{1,0:T(8,128)(2,1)S(1)} %add_convert_fusion.5), channel_id=1, source_target_pairs={{0,2},{1,7},{2,4},{3,1},{4,6},{5,3},{6,0},{7,5},{8,10},{9,15},{10,... | collective-permute-start | bytes 1966088 | tf_op jit(solution)/shard_map/ppermute | solution.py:174
  192.3 13.3 %collective-permute-start.6 = (bf16[256,1280]{1,0:T(8,128)(2,1)S(1)}, bf16[256,1280]{1,0:T(8,128)(2,1)S(1)}, u32[]{:S(2)}, u32[]{:S(2)}) collective-permute-start(bf16[256,1280]{1,0:T(8,128)(2,1)S(1)} %add_convert_fusion.2), channel_id=1, source_target_pairs={{0,2},{1,7},{2,4},{3,1},{4,6},{5,3},{6,0},{7,5},{8,10},{9,15},{10,... | collective-permute-start | bytes 1966088 | tf_op jit(solution)/shard_map/ppermute | solution.py:174
  199.3 13.3 %collective-permute-start.4 = (bf16[256,1280]{1,0:T(8,128)(2,1)S(1)}, bf16[256,1280]{1,0:T(8,128)(2,1)S(1)}, u32[]{:S(2)}, u32[]{:S(2)}) collective-permute-start(bf16[256,1280]{1,0:T(8,128)(2,1)S(1)} %add_convert_fusion.4), channel_id=1, source_target_pairs={{0,2},{1,7},{2,4},{3,1},{4,6},{5,3},{6,0},{7,5},{8,10},{9,15},{10,... | collective-permute-start | bytes 1966088 | tf_op jit(solution)/shard_map/ppermute | solution.py:174
  206.3 13.3 %collective-permute-start.7 = (bf16[256,1280]{1,0:T(8,128)(2,1)S(1)}, bf16[256,1280]{1,0:T(8,128)(2,1)S(1)}, u32[]{:S(2)}, u32[]{:S(2)}) collective-permute-start(bf16[256,1280]{1,0:T(8,128)(2,1)S(1)} %add_convert_fusion.1), channel_id=1, source_target_pairs={{0,2},{1,7},{2,4},{3,1},{4,6},{5,3},{6,0},{7,5},{8,10},{9,15},{10,... | collective-permute-start | bytes 1966088 | tf_op jit(solution)/shard_map/ppermute | solution.py:174
  220.4 6.2 %copy-start.4 = (s32[16,3]{0,1:T(4,128)S(1)}, s32[16,3]{0,1:T(4,128)}, u32[]{:S(2)}) copy-start(s32[16,3]{0,1:T(4,128)} %param.12) | copy-start | bytes 580
  220.4 6.3 %copy-start.5 = (f32[16,3]{0,1:T(4,128)S(1)}, f32[16,3]{0,1:T(4,128)}, u32[]{:S(2)}) copy-start(f32[16,3]{0,1:T(4,128)} %param.13) | copy-start | bytes 580
  221.6 25.5 %all-to-all-start.3 = ((bf16[16,16,2560]{2,1,0:T(8,128)(2,1)}), bf16[16,16,2560]{2,1,0:T(8,128)(2,1)S(1)}, u32[]{:S(2)}, u32[]{:S(2)}) async-start(bf16[16,16,2560]{2,1,0:T(8,128)(2,1)} %bitcast.21), calls=%async_computation.4 | async-start | bytes 2621440 | tf_op jit(solution)/shard_map/all_to_all | solution.py:179
  226.6 45.2 %copy-start.3 = (bf16[16,7168]{1,0:T(8,128)(2,1)S(1)}, bf16[16,7168]{1,0:T(8,128)(2,1)}, u32[]{:S(2)}) copy-start(bf16[16,7168]{1,0:T(8,128)(2,1)} %hidden_ref.1) | copy-start | bytes 688132
  256.4 14.9 %all-to-all-start.2 = ((bf16[8,8,4608]{2,1,0:T(8,128)(2,1)}), bf16[8,8,4608]{2,1,0:T(8,128)(2,1)S(1)}, u32[]{:S(2)}, u32[]{:S(2)}) async-start(bf16[8,8,4608]{2,1,0:T(8,128)(2,1)} %bitcast.45), calls=%async_computation.3 | async-start | bytes 1179648 | tf_op jit(solution)/shard_map/all_to_all | solution.py:250
  273.1 15.5 %all-to-all-start.4 = ((bf16[16,2,7168]{2,1,0:T(2,128)(2,1)}), bf16[16,2,7168]{2,1,0:T(2,128)(2,1)S(1)}, u32[]{:S(2)}, u32[]{:S(2)}) async-start(bf16[16,2,7168]{2,1,0:T(2,128)(2,1)} %all_to_all.24), calls=%async_computation.5 | async-start | bytes 917504 | tf_op jit(solution)/shard_map/all_to_all | solution.py:277
  278.0 11.5 %copy-start.1 = (bf16[32,64,512]{2,1,0:T(8,128)(2,1)S(1)}, bf16[32,64,512]{2,1,0:T(8,128)(2,1)}, u32[]{:S(2)}) copy-start(bf16[32,64,512]{2,1,0:T(8,128)(2,1)} %param.16) | copy-start | bytes 6291460
Sparse Core Ops, SparseCore 0:
  11.6 114.1 all-gather.1
  166.3 90.0 reduce-scatter.1

commit v7 on v6

--- a/solution.py
+++ b/solution.py
@@ -113,7 +113,7 @@
     slots = count // req_dev * cap
     group = 16 * req_dev
     groups = count // group
-    up, down = width // 7, 1536
+    up, down = width // 7, 2304
     up_steps, down_steps = width // up, main // down
 
     def at_up(s):

time: 297 us -> 297 us (level)
  no operation moved by 1% of the time
where the time goes in v7:
time: 297 us
  waiting for transfers between devices  149 us (50%)
  blocking collectives  37.5 us (13%)
  Pallas kernels  33.6 us (11%)
  starting transfers between devices  22.7 us (8%)
  other arithmetic  18.5 us (6%)
  between operations  14.3 us (5%)
  local copies, waits for them, and re-layouts  12.8 us (4%)
  matrix products  8.05 us (3%)
    all_gather x1, waiting for transfers between devices, body(): gathered = lax.all_gather(payload, ('attn', 'ffn'), axis=0, tiled=True)  58.2 us
    ppermute x6, waiting for transfers between devices, ring_sum(): arrived = lax.ppermute(total.astype(jnp.bfloat16), 'ffn', ring)  41 us
    all_to_all x1, blocking collectives, body(): lax.all_to_all(pages_out(kv_pages, 0), 'attn', split_axis=0, concat_axis=...  37.5 us
    pallas_call x1, Pallas kernels, run_experts(): pl.pallas_call(functools.partial(expert_kernel, hidden_dev, req_dev, cap,...  31.6 us
    all_to_all x1, waiting for transfers between devices, reduce_side(): lax.all_to_all(total.reshape(instances, req_dev, cols), 'attn', split_axi...  20 us
    all_to_all x1, waiting for transfers between devices, body(): lax.all_to_all(results, 'ffn', split_axis=0, concat_axis=0, tiled=True)  10.6 us
    reduce_scatter x1, waiting for transfers between devices, body(): summed = lax.psum_scatter(partial, 'attn', scatter_dimension=0, tiled=True)  9.08 us
    dot_general x8, matrix products, part(): jnp.dot(rows, weight_out[:, span], preferred_element_type=jnp.float32)  7.25 us
  transfers between devices with their start and end apart: 14, of which 13 were waited for; matrix products, arithmetic and copies ran while one was open for 12% of the time, Pallas kernels for 11%

profile of v7, /device:TPU:0, one launch (start us, length us, event | category | flops | bytes accessed | tf_op | source)
XLA Modules:
  0.0 296.6 jit_solution(6225519050585579227)
XLA Ops:
  7.2 2.0 shard_map.113
  13.2 1.4 gather_fusion
  14.7 2.0 gather_fusion.2
  16.9 1.8 broadcast_select_fusion.1
  18.7 37.5 %all_to_all.32 = bf16[32,64,512]{2,1,0:T(8,128)(2,1)} all-to-all(bf16[32,64,512]{2,1,0:T(8,128)(2,1)S(1)} %broadcast_select_fusion.1), channel_id=1, replica_groups=mesh['attn'=16,'ffn'=8] {'attn'}, dimensions={0} | all-to-all | bytes 4194304 | tf_op jit(solution)/shard_map/all_to_all | solution.py:228
  56.2 2.7 slice.36
  59.0 2.0 gather_fusion.3
  61.0 2.8 broadcast_select_fusion
  63.7 3.9 %pad_maximum_fusion.1 = bf16[640,2560]{1,0:T(8,128)(2,1)} fusion(bf16[320,2560]{1,0:T(8,128)(2,1)} %collective-permute-done, bf16[320,2560]{1,0:T(8,128)(2,1)} %slice.36), kind=kLoop, calls=%fused_computation.6 | loop fusion | flops 6553600 | bytes 6553600 | tf_op jit(solution)/shard_map/concatenate | solution.py:236
  67.7 58.2 %all-gather.2.cloned.1.call-done.lanes_ref.rows_ref = bf16[2048,7296]{1,0:T(8,128)(2,1)} async-done(((bf16[16,7296]{1,0:T(8,128)(2,1)}), bf16[2048,7296]{1,0:T(8,128)(2,1)}) %all-gather.2.cloned.1.call-update) | async-done | bytes 29884432 | tf_op jit(solution)/shard_map/all_gather | solution.py:208
  125.8 6.8 %all-to-all-start.1 = ((bf16[32,64,512]{2,1,0:T(8,128)(2,1)}), bf16[32,64,512]{2,1,0:T(8,128)(2,1)}, u32[]{:S(2)}, u32[]{:S(2)}) async-start(bf16[32,64,512]{2,1,0:T(8,128)(2,1)} %broadcast_select_fusion), calls=%async_computation.1 | async-start | bytes 4194304 | tf_op jit(solution)/shard_map/all_to_all | solution.py:240
  132.7 31.6 %shard_map.114 = (bf16[1024,4608]{1,0:T(8,128)(2,1)}, bf16[2048,320]{1,0:T(8,128)(2,1)S(1)}) custom-call(s32[1]{0:T(128)} %bitcast.9.member_ref, bf16[2048,7296]{1,0:T(8,128)(2,1)} %all-gather.2.cloned.1.call-done.lanes_ref.rows_ref, bf16[2048,7296]{1,0:T(8,128)(2,1)} %all-gather.2.cloned.1.call-done.lanes_ref.rows_ref, bf16[640,7168]{1,0:T(8,128)(2,1)} %bitcast.41, ...), custom_call_target="tpu_custom_call" | custom-call | flops 16173236224 | bytes 52756480 | tf_op jit(solution)/shard_map/pallas_call | solution.py:125
  164.3 1.9 all-to-all-done.1
  166.2 1.1 dynamic-slice_bitcast_fusion
  167.3 2.5 collective-permute-done.1
  170.3 2.4 convolution_convert_fusion.2
  173.7 1.3 collective-permute-start.5
  175.0 9.8 %collective-permute-done.2 = bf16[256,1280]{1,0:T(8,128)(2,1)S(1)} collective-permute-done((bf16[256,1280]{1,0:T(8,128)(2,1)S(1)}, bf16[256,1280]{1,0:T(8,128)(2,1)S(1)}, u32[]{:S(2)}, u32[]{:S(2)}) %collective-permute-start.2) | collective-permute-done | bytes 655392 | tf_op jit(solution)/shard_map/ppermute | solution.py:174
  185.5 6.2 %collective-permute-done.5 = bf16[256,1280]{1,0:T(8,128)(2,1)S(1)} collective-permute-done((bf16[256,1280]{1,0:T(8,128)(2,1)S(1)}, bf16[256,1280]{1,0:T(8,128)(2,1)S(1)}, u32[]{:S(2)}, u32[]{:S(2)}) %collective-permute-start.5) | collective-permute-done | bytes 655392 | tf_op jit(solution)/shard_map/ppermute | solution.py:174
  192.6 6.2 %collective-permute-done.3 = bf16[256,1280]{1,0:T(8,128)(2,1)S(1)} collective-permute-done((bf16[256,1280]{1,0:T(8,128)(2,1)S(1)}, bf16[256,1280]{1,0:T(8,128)(2,1)S(1)}, u32[]{:S(2)}, u32[]{:S(2)}) %collective-permute-start.3) | collective-permute-done | bytes 655392 | tf_op jit(solution)/shard_map/ppermute | solution.py:174
  199.6 6.2 %collective-permute-done.6 = bf16[256,1280]{1,0:T(8,128)(2,1)S(1)} collective-permute-done((bf16[256,1280]{1,0:T(8,128)(2,1)S(1)}, bf16[256,1280]{1,0:T(8,128)(2,1)S(1)}, u32[]{:S(2)}, u32[]{:S(2)}) %collective-permute-start.6) | collective-permute-done | bytes 655392 | tf_op jit(solution)/shard_map/ppermute | solution.py:174
  206.6 6.2 %collective-permute-done.4 = bf16[256,1280]{1,0:T(8,128)(2,1)S(1)} collective-permute-done((bf16[256,1280]{1,0:T(8,128)(2,1)S(1)}, bf16[256,1280]{1,0:T(8,128)(2,1)S(1)}, u32[]{:S(2)}, u32[]{:S(2)}) %collective-permute-start.4) | collective-permute-done | bytes 655392 | tf_op jit(solution)/shard_map/ppermute | solution.py:174
  213.5 6.3 %collective-permute-done.7 = bf16[256,1280]{1,0:T(8,128)(2,1)S(1)} collective-permute-done((bf16[256,1280]{1,0:T(8,128)(2,1)S(1)}, bf16[256,1280]{1,0:T(8,128)(2,1)S(1)}, u32[]{:S(2)}, u32[]{:S(2)}) %collective-permute-start.7) | collective-permute-done | bytes 655392 | tf_op jit(solution)/shard_map/ppermute | solution.py:174
  220.6 1.1 pad_maximum_fusion.2
  221.7 5.3 %all-to-all-start.3 = ((bf16[16,16,2560]{2,1,0:T(8,128)(2,1)}), bf16[16,16,2560]{2,1,0:T(8,128)(2,1)S(1)}, u32[]{:S(2)}, u32[]{:S(2)}) async-start(bf16[16,16,2560]{2,1,0:T(8,128)(2,1)} %bitcast.21), calls=%async_computation.4 | async-start | bytes 2621440 | tf_op jit(solution)/shard_map/all_to_all | solution.py:179
  227.7 20.0 %all-to-all-done.3 = bf16[16,16,2560]{2,1,0:T(8,128)(2,1)S(1)} async-done(((bf16[16,16,2560]{2,1,0:T(8,128)(2,1)}), bf16[16,16,2560]{2,1,0:T(8,128)(2,1)S(1)}, u32[]{:S(2)}, u32[]{:S(2)}) %all-to-all-start.3) | async-done | bytes 1310752 | tf_op jit(solution)/shard_map/all_to_all | solution.py:179
  247.8 9.1 %reduce-scatter.2.cloned.1.call-done = bf16[64,4608]{1,0:T(8,128)(2,1)} async-done(((bf16[1024,4608]{1,0:T(8,128)(2,1)}), bf16[64,4608]{1,0:T(8,128)(2,1)}) %reduce-scatter.2.cloned.1.call-update) | async-done | bytes 589840 | tf_op jit(solution)/shard_map/reduce_scatter | solution.py:248
  256.9 3.8 %all-to-all-start.2 = ((bf16[8,8,4608]{2,1,0:T(8,128)(2,1)}), bf16[8,8,4608]{2,1,0:T(8,128)(2,1)S(1)}, u32[]{:S(2)}, u32[]{:S(2)}) async-start(bf16[8,8,4608]{2,1,0:T(8,128)(2,1)} %bitcast.45), calls=%async_computation.3 | async-start | bytes 1179648 | tf_op jit(solution)/shard_map/all_to_all | solution.py:250
  261.1 10.6 %all-to-all-done.2 = bf16[8,8,4608]{2,1,0:T(8,128)(2,1)S(1)} async-done(((bf16[8,8,4608]{2,1,0:T(8,128)(2,1)}), bf16[8,8,4608]{2,1,0:T(8,128)(2,1)S(1)}, u32[]{:S(2)}, u32[]{:S(2)}) %all-to-all-start.2) | async-done | bytes 589856 | tf_op jit(solution)/shard_map/all_to_all | solution.py:250
  273.5 4.8 %all-to-all-start.4 = ((bf16[16,2,7168]{2,1,0:T(2,128)(2,1)}), bf16[16,2,7168]{2,1,0:T(2,128)(2,1)S(1)}, u32[]{:S(2)}, u32[]{:S(2)}) async-start(bf16[16,2,7168]{2,1,0:T(2,128)(2,1)} %all_to_all.24), calls=%async_computation.5 | async-start | bytes 917504 | tf_op jit(solution)/shard_map/all_to_all | solution.py:277
  278.3 4.8 %pad_maximum_fusion = bf16[32,2,64,512]{3,2,1,0:T(8,128)(2,1)} fusion(bf16[32,1,64,512]{3,2,1,0:T(8,128)(2,1)} %bitcast.11, bf16[32,1,64,512]{3,2,1,0:T(8,128)(2,1)} %bitcast.44), kind=kLoop, calls=%fused_computation.5 | loop fusion | flops 2097152 | bytes 8388608 | tf_op jit(solution)/shard_map/stack | solution.py:247
  283.1 5.8 %all-to-all-done.4 = bf16[16,2,7168]{2,1,0:T(2,128)(2,1)S(1)} async-done(((bf16[16,2,7168]{2,1,0:T(2,128)(2,1)}), bf16[16,2,7168]{2,1,0:T(2,128)(2,1)S(1)}, u32[]{:S(2)}, u32[]{:S(2)}) %all-to-all-start.4) | async-done | bytes 458784 | tf_op jit(solution)/shard_map/all_to_all | solution.py:277
  (61 shorter events, 14.1 us)
Async XLA Ops:
  7.2 7.5 %copy-start = (bf16[32,64,512]{2,1,0:T(8,128)(2,1)S(1)}, bf16[32,64,512]{2,1,0:T(8,128)(2,1)}, u32[]{:S(2)}) copy-start(bf16[32,64,512]{2,1,0:T(8,128)(2,1)} %param.16) | copy-start | bytes 6291460
  7.2 118.7 %all-gather.2.cloned.1.call-start = ((), (), s32[]{:S(2)}) async-start(), calls=%async_computation.6 | async-start | bytes 30117888 | tf_op jit(solution)/shard_map/all_gather | solution.py:208
  59.0 4.8 %collective-permute-start = (bf16[320,2560]{1,0:T(8,128)(2,1)}, bf16[320,2560]{1,0:T(8,128)(2,1)}, u32[]{:S(2)}, u32[]{:S(2)}) collective-permute-start(bf16[320,2560]{1,0:T(8,128)(2,1)} %slice.36), channel_id=1, source_target_pairs={{0,1},{1,0},{2,3},{3,2},{4,5},{5,4},{6,7},{7,6},{8,9},{9,8},{10,11... | collective-permute-start | bytes 4915208 | tf_op jit(solution)/shard_map/ppermute | solution.py:236
  125.8 40.4 %all-to-all-start.1 = ((bf16[32,64,512]{2,1,0:T(8,128)(2,1)}), bf16[32,64,512]{2,1,0:T(8,128)(2,1)}, u32[]{:S(2)}, u32[]{:S(2)}) async-start(bf16[32,64,512]{2,1,0:T(8,128)(2,1)} %broadcast_select_fusion), calls=%async_computation.1 | async-start | bytes 4194304 | tf_op jit(solution)/shard_map/all_to_all | solution.py:240
  132.7 124.2 %reduce-scatter.2.cloned.1.call-start = ((), (), s32[]{:S(2)}) async-start(), calls=%async_computation.7 | async-start | bytes 10027008 | tf_op jit(solution)/shard_map/reduce_scatter | solution.py:248
  167.3 2.5 collective-permute-start.1
  169.8 3.2 %copy-start.2 = (bf16[640,2560]{1,0:T(8,128)(2,1)S(1)}, bf16[640,2560]{1,0:T(8,128)(2,1)}, u32[]{:S(2)}) copy-start(bf16[640,2560]{1,0:T(8,128)(2,1)} %pad_maximum_fusion.1) | copy-start | bytes 9830404
  172.7 12.0 %collective-permute-start.2 = (bf16[256,1280]{1,0:T(8,128)(2,1)S(1)}, bf16[256,1280]{1,0:T(8,128)(2,1)S(1)}, u32[]{:S(2)}, u32[]{:S(2)}) collective-permute-start(bf16[256,1280]{1,0:T(8,128)(2,1)S(1)} %convolution_convert_fusion.2), channel_id=1, source_target_pairs={{0,2},{1,7},{2,4},{3,1},{4,6},{5,3},{6,0},{7,5},{8,10},{9,15},{10,... | collective-permute-start | bytes 1966088 | tf_op jit(solution)/shard_map/ppermute | solution.py:174
  173.7 18.1 %collective-permute-start.5 = (bf16[256,1280]{1,0:T(8,128)(2,1)S(1)}, bf16[256,1280]{1,0:T(8,128)(2,1)S(1)}, u32[]{:S(2)}, u32[]{:S(2)}) collective-permute-start(bf16[256,1280]{1,0:T(8,128)(2,1)S(1)} %convolution_convert_fusion.1), channel_id=1, source_target_pairs={{0,2},{1,7},{2,4},{3,1},{4,6},{5,3},{6,0},{7,5},{8,10},{9,15},{10,... | collective-permute-start | bytes 1966088 | tf_op jit(solution)/shard_map/ppermute | solution.py:174
  185.5 13.3 %collective-permute-start.3 = (bf16[256,1280]{1,0:T(8,128)(2,1)S(1)}, bf16[256,1280]{1,0:T(8,128)(2,1)S(1)}, u32[]{:S(2)}, u32[]{:S(2)}) collective-permute-start(bf16[256,1280]{1,0:T(8,128)(2,1)S(1)} %add_convert_fusion.5), channel_id=1, source_target_pairs={{0,2},{1,7},{2,4},{3,1},{4,6},{5,3},{6,0},{7,5},{8,10},{9,15},{10,... | collective-permute-start | bytes 1966088 | tf_op jit(solution)/shard_map/ppermute | solution.py:174
  192.5 13.3 %collective-permute-start.6 = (bf16[256,1280]{1,0:T(8,128)(2,1)S(1)}, bf16[256,1280]{1,0:T(8,128)(2,1)S(1)}, u32[]{:S(2)}, u32[]{:S(2)}) collective-permute-start(bf16[256,1280]{1,0:T(8,128)(2,1)S(1)} %add_convert_fusion.2), channel_id=1, source_target_pairs={{0,2},{1,7},{2,4},{3,1},{4,6},{5,3},{6,0},{7,5},{8,10},{9,15},{10,... | collective-permute-start | bytes 1966088 | tf_op jit(solution)/shard_map/ppermute | solution.py:174
  199.5 13.3 %collective-permute-start.4 = (bf16[256,1280]{1,0:T(8,128)(2,1)S(1)}, bf16[256,1280]{1,0:T(8,128)(2,1)S(1)}, u32[]{:S(2)}, u32[]{:S(2)}) collective-permute-start(bf16[256,1280]{1,0:T(8,128)(2,1)S(1)} %add_convert_fusion.4), channel_id=1, source_target_pairs={{0,2},{1,7},{2,4},{3,1},{4,6},{5,3},{6,0},{7,5},{8,10},{9,15},{10,... | collective-permute-start | bytes 1966088 | tf_op jit(solution)/shard_map/ppermute | solution.py:174
  206.5 13.3 %collective-permute-start.7 = (bf16[256,1280]{1,0:T(8,128)(2,1)S(1)}, bf16[256,1280]{1,0:T(8,128)(2,1)S(1)}, u32[]{:S(2)}, u32[]{:S(2)}) collective-permute-start(bf16[256,1280]{1,0:T(8,128)(2,1)S(1)} %add_convert_fusion.1), channel_id=1, source_target_pairs={{0,2},{1,7},{2,4},{3,1},{4,6},{5,3},{6,0},{7,5},{8,10},{9,15},{10,... | collective-permute-start | bytes 1966088 | tf_op jit(solution)/shard_map/ppermute | solution.py:174
  220.6 6.5 %copy-start.4 = (s32[16,3]{0,1:T(4,128)S(1)}, s32[16,3]{0,1:T(4,128)}, u32[]{:S(2)}) copy-start(s32[16,3]{0,1:T(4,128)} %param.12) | copy-start | bytes 580
  220.6 6.6 %copy-start.5 = (f32[16,3]{0,1:T(4,128)S(1)}, f32[16,3]{0,1:T(4,128)}, u32[]{:S(2)}) copy-start(f32[16,3]{0,1:T(4,128)} %param.13) | copy-start | bytes 580
  221.7 26.0 %all-to-all-start.3 = ((bf16[16,16,2560]{2,1,0:T(8,128)(2,1)}), bf16[16,16,2560]{2,1,0:T(8,128)(2,1)S(1)}, u32[]{:S(2)}, u32[]{:S(2)}) async-start(bf16[16,16,2560]{2,1,0:T(8,128)(2,1)} %bitcast.21), calls=%async_computation.4 | async-start | bytes 2621440 | tf_op jit(solution)/shard_map/all_to_all | solution.py:179
  227.1 45.1 %copy-start.3 = (bf16[16,7168]{1,0:T(8,128)(2,1)S(1)}, bf16[16,7168]{1,0:T(8,128)(2,1)}, u32[]{:S(2)}) copy-start(bf16[16,7168]{1,0:T(8,128)(2,1)} %hidden_ref.1) | copy-start | bytes 688132
  256.9 14.9 %all-to-all-start.2 = ((bf16[8,8,4608]{2,1,0:T(8,128)(2,1)}), bf16[8,8,4608]{2,1,0:T(8,128)(2,1)S(1)}, u32[]{:S(2)}, u32[]{:S(2)}) async-start(bf16[8,8,4608]{2,1,0:T(8,128)(2,1)} %bitcast.45), calls=%async_computation.3 | async-start | bytes 1179648 | tf_op jit(solution)/shard_map/all_to_all | solution.py:250
  273.5 15.4 %all-to-all-start.4 = ((bf16[16,2,7168]{2,1,0:T(2,128)(2,1)}), bf16[16,2,7168]{2,1,0:T(2,128)(2,1)S(1)}, u32[]{:S(2)}, u32[]{:S(2)}) async-start(bf16[16,2,7168]{2,1,0:T(2,128)(2,1)} %all_to_all.24), calls=%async_computation.5 | async-start | bytes 917504 | tf_op jit(solution)/shard_map/all_to_all | solution.py:277
  278.3 11.5 %copy-start.1 = (bf16[32,64,512]{2,1,0:T(8,128)(2,1)S(1)}, bf16[32,64,512]{2,1,0:T(8,128)(2,1)}, u32[]{:S(2)}) copy-start(bf16[32,64,512]{2,1,0:T(8,128)(2,1)} %param.16) | copy-start | bytes 6291460
Sparse Core Ops, SparseCore 0:
  11.6 114.1 all-gather.1
  166.3 90.4 reduce-scatter.1
